TPU v7x, 128 devices: a whole 4x4x4 slice. The times are simulated.
128 devices in a mesh: dp: 4 (over z), head: 32 (over y, x, core).
Axes of the slice: x: 4, y: 4, z: 4, core: 2. Of those that a mesh axis runs over, the one named last changes fastest.
Arguments:
- queries: bfloat16 [24576, 4096], P(('dp', 'head')), parts along dimension 0, may hold values from -6 to 6
- key_vectors: bfloat16 [24576, 4096], P(('dp', 'head')), parts along dimension 0, may hold values from -6 to 6
- values: bfloat16 [24576, 4096], P(('dp', 'head')), parts along dimension 0, may hold values from -6 to 6
- out_grad: bfloat16 [24576, 4096], P(('dp', 'head')), parts along dimension 0, may hold values from -6 to 6
- output: bfloat16 [24576, 4096], P(('dp', 'head')), parts along dimension 0, may hold values from -3 to 3
- key_blocks: int32 [128, 48, 12], P(('dp', 'head')), parts along dimension 0, may hold values from 0 to 47, as said below
- block_count: int32 [128, 48], P(('dp', 'head')), parts along dimension 0, may hold values from 2 to 12, as said below
Outputs:
- query_grad: bfloat16 [24576, 4096], P(('dp', 'head')), parts along dimension 0
- key_grad: bfloat16 [24576, 4096], P(('dp', 'head')), parts along dimension 0
- value_grad: bfloat16 [24576, 4096], P(('dp', 'head')), parts along dimension 0
There are 4 independent parts, one for each index of `dp`. A program takes and returns all parts, laid end to end along the dimension named above; each array names one. Nothing has to cross between parts.
Inputs may be any that keep to these rules, and one draw needn't show every extreme that they name: `key_blocks`: slot 0 of every query block names the block itself; the live slots of one query block name different blocks; slots at or past block_count hold block numbers that are ignored. `block_count`: every head has a query block with exactly 12 live slots.
All inputs are finite; a program needn't handle non-finite values.
Results may differ from a plain program's by a relative error of at most 0.0049.
Values may be sent and summed in bfloat16 or wider, within the bound.
No kernel may reach another device: no remote copies, remote signals or barrier semaphores. Data moves between devices by JAX's collectives and lax.ppermute only.
A program may use at most 128 MiB of HBM per device.

v0:
```python
import jax
import jax.numpy as jnp
from jax import lax
from jax.sharding import PartitionSpec as P

HD = 128
BLK = 128


def pick_group():
    for size_try in (8, 4, 2, 1):
        return size_try
    return 1


def head_gradients(queries, key_vectors, values, out_grad, row_terms, key_blocks, block_count):
    blocks_total = queries.shape[0] // BLK
    slots = key_blocks.shape[1]
    group = pick_group()
    steps_total = blocks_total // group
    scale_factor = HD ** (-0.5)
    tile_width = BLK * HD
    both_tiles = jnp.concatenate(
        [key_vectors.reshape(blocks_total, tile_width), values.reshape(blocks_total, tile_width)],
        axis=1,
    )
    stacked = (
        queries.reshape(steps_total, group, BLK, HD),
        out_grad.reshape(steps_total, group, BLK, HD),
        row_terms.reshape(steps_total, group, BLK),
        key_blocks.reshape(steps_total, group, slots),
        block_count.reshape(steps_total, group),
    )
    block_ids = jnp.arange(blocks_total, dtype=jnp.int32)

    def one_step(carry, items):
        query_tile, grad_tile, term_tile, index_tile, count_tile = items
        flat_index = index_tile.reshape(-1)
        selector = flat_index[:, None] == block_ids[None, :]
        picked = jnp.dot(
            selector.astype(jnp.bfloat16), both_tiles, preferred_element_type=jnp.float32
        ).astype(jnp.bfloat16)
        chosen_keys = picked[:, :tile_width].reshape(group, slots, BLK, HD)
        chosen_values = picked[:, tile_width:].reshape(group, slots, BLK, HD)
        scores = (
            jnp.einsum(
                "gqd,gkjd->gqkj", query_tile, chosen_keys, preferred_element_type=jnp.float32
            )
            * scale_factor
        )
        slot_ids = jnp.arange(slots, dtype=jnp.int32)
        live = slot_ids[None, :] < count_tile[:, None]
        scores = jnp.where(live[:, None, :, None], scores, -1e30)
        top = jnp.max(scores, axis=(2, 3), keepdims=True)
        weights = jnp.exp(scores - top)
        probs = weights / jnp.sum(weights, axis=(2, 3), keepdims=True)
        probs_low = probs.astype(jnp.bfloat16)
        value_part = jnp.einsum(
            "gqkj,gqd->gkjd", probs_low, grad_tile, preferred_element_type=jnp.float32
        )
        prob_grad = jnp.einsum(
            "gqd,gkjd->gqkj", grad_tile, chosen_values, preferred_element_type=jnp.float32
        )
        score_grad = (probs * (prob_grad - term_tile[:, :, None, None])).astype(jnp.bfloat16)
        query_part = (
            jnp.einsum(
                "gqkj,gkjd->gqd", score_grad, chosen_keys, preferred_element_type=jnp.float32
            )
            * scale_factor
        )
        key_part = (
            jnp.einsum("gqkj,gqd->gkjd", score_grad, query_tile, preferred_element_type=jnp.float32)
            * scale_factor
        )
        parts_both = jnp.concatenate(
            [key_part.reshape(-1, tile_width), value_part.reshape(-1, tile_width)], axis=1
        )
        added = lax.dot_general(
            selector.astype(jnp.float32),
            parts_both,
            (((0,), (0,)), ((), ())),
            precision=lax.Precision.HIGHEST,
            preferred_element_type=jnp.float32,
        )
        return (carry + added, query_part.astype(jnp.bfloat16))

    start_acc = jnp.zeros((blocks_total, 2 * tile_width), jnp.float32)
    both_acc, query_parts = lax.scan(one_step, start_acc, stacked)
    total_rows = blocks_total * BLK
    return (
        query_parts.reshape(total_rows, HD),
        both_acc[:, :tile_width].reshape(total_rows, HD).astype(jnp.bfloat16),
        both_acc[:, tile_width:].reshape(total_rows, HD).astype(jnp.bfloat16),
    )


def per_device(queries, key_vectors, values, out_grad, output, key_blocks, block_count):
    heads_here = key_blocks.shape[0]
    head_query, head_keys, head_values, head_grad, head_output = (
        lax.all_to_all(queries, "head", split_axis=1, concat_axis=0, tiled=True),
        lax.all_to_all(key_vectors, "head", split_axis=1, concat_axis=0, tiled=True),
        lax.all_to_all(values, "head", split_axis=1, concat_axis=0, tiled=True),
        lax.all_to_all(out_grad, "head", split_axis=1, concat_axis=0, tiled=True),
        lax.all_to_all(output, "head", split_axis=1, concat_axis=0, tiled=True),
    )
    tokens_total = head_query.shape[0]
    products = head_grad.astype(jnp.float32) * head_output.astype(jnp.float32)
    row_terms = jnp.sum(products.reshape(tokens_total, heads_here, HD), axis=-1)
    results = head_gradients(
        head_query,
        head_keys,
        head_values,
        head_grad,
        row_terms[:, 0],
        key_blocks[0],
        block_count[0],
    )
    query_list = results[0]
    key_list = results[1]
    value_list = results[2]
    query_grad, key_grad, value_grad = (
        lax.all_to_all(query_list, "head", split_axis=0, concat_axis=1, tiled=True),
        lax.all_to_all(key_list, "head", split_axis=0, concat_axis=1, tiled=True),
        lax.all_to_all(value_list, "head", split_axis=0, concat_axis=1, tiled=True),
    )
    return (query_grad, key_grad, value_grad)


def solution(mesh):
    in_specs = (
        P(("dp", "head"), None),
        P(("dp", "head"), None),
        P(("dp", "head"), None),
        P(("dp", "head"), None),
        P(("dp", "head"), None),
        P(("dp", "head"), None, None),
        P(("dp", "head"), None),
    )
    out_specs = (P(("dp", "head"), None), P(("dp", "head"), None), P(("dp", "head"), None))
    return jax.shard_map(
        per_device, mesh=mesh, in_specs=in_specs, out_specs=out_specs, check_vma=False
    )
```

profile of v0, /device:TPU:0, one launch (start us, length us, event | category | flops | bytes accessed | tf_op | source)
XLA Modules:
  0.0 554.8 jit_solution(8809726561858006808)
XLA Ops:
  3.6 7.5 %all-to-all-start.1 = ((bf16[192,32,128]{2,0,1:T(8,128)(2,1)}), bf16[192,32,128]{2,0,1:T(8,128)(2,1)S(1)}, u32[]{:S(2)}, u32[]{:S(2)}) async-start(bf16[192,32,128]{2,0,1:T(8,128)(2,1)} %copy_bitcast_fusion.8), calls=%async_computation.1 | async-start | bytes 3145728 | tf_op jit(solution)/shard_map/all_to_all | solution.py:101
  12.8 22.3 %all-to-all-done.1 = bf16[192,32,128]{2,0,1:T(8,128)(2,1)S(1)} async-done(((bf16[192,32,128]{2,0,1:T(8,128)(2,1)}), bf16[192,32,128]{2,0,1:T(8,128)(2,1)S(1)}, u32[]{:S(2)}, u32[]{:S(2)}) %all-to-all-start.1) | async-done | bytes 1572896 | tf_op jit(solution)/shard_map/all_to_all | solution.py:101
  35.1 4.0 all-to-all-start.2
  39.1 3.0 copy_bitcast_fusion.6
  42.1 20.9 %all-to-all-done.2 = bf16[192,32,128]{2,0,1:T(8,128)(2,1)S(1)} async-done(((bf16[192,32,128]{2,0,1:T(8,128)(2,1)}), bf16[192,32,128]{2,0,1:T(8,128)(2,1)S(1)}, u32[]{:S(2)}, u32[]{:S(2)}) %all-to-all-start.2) | async-done | bytes 1572896 | tf_op jit(solution)/shard_map/all_to_all | solution.py:102
  64.2 4.0 all-to-all-start.3
  68.2 3.1 copy_bitcast_fusion.5
  71.3 20.8 %all-to-all-done.3 = bf16[192,32,128]{2,0,1:T(8,128)(2,1)S(1)} async-done(((bf16[192,32,128]{2,0,1:T(8,128)(2,1)}), bf16[192,32,128]{2,0,1:T(8,128)(2,1)S(1)}, u32[]{:S(2)}, u32[]{:S(2)}) %all-to-all-start.3) | async-done | bytes 1572896 | tf_op jit(solution)/shard_map/all_to_all | solution.py:103
  92.1 4.7 all-to-all-start.4
  98.2 3.0 copy_bitcast_fusion.9
  101.1 2.0 reshape.104
  103.2 2.0 reshape.105
  105.2 15.5 %all-to-all-done.4 = bf16[192,32,128]{2,0,1:T(8,128)(2,1)} async-done(((bf16[192,32,128]{2,0,1:T(8,128)(2,1)}), bf16[192,32,128]{2,0,1:T(8,128)(2,1)}, u32[]{:S(2)}, u32[]{:S(2)}) %all-to-all-start.4) | async-done | bytes 1572896 | tf_op jit(solution)/shard_map/all_to_all | solution.py:104
  120.7 4.7 all-to-all-start
  125.4 2.2 pad_maximum_fusion
  127.8 2.6 fusion.34
  130.4 18.9 %all-to-all-done = bf16[192,32,128]{2,0,1:T(8,128)(2,1)} async-done(((bf16[192,32,128]{2,0,1:T(8,128)(2,1)}), bf16[192,32,128]{2,0,1:T(8,128)(2,1)}, u32[]{:S(2)}, u32[]{:S(2)}) %all-to-all-start) | async-done | bytes 1572896 | tf_op jit(solution)/shard_map/all_to_all | solution.py:100
  149.3 317.5 %while.13 = (s32[]{:T(128)}, f32[48,32768]{1,0:T(8,128)}, bf16[6,8,128,128]{3,2,1,0:T(8,128)(2,1)}, s32[6,8,12]{2,1,0:T(8,128)S(1)}, s32[6,8]{1,0:T(8,128)S(1)},...) while((s32[]{:T(128)}, f32[48,32768]{1,0:T(8,128)}, ...), condition=%wide.region_4.5_spmd.clone, body=%wide.region_1.4_spmd.clone.sunk | while | flops 4168358912 | bytes 168078384 | solution.py:88
  153.8 2.0 fusion.78
  157.3 3.2 multiply_convert_fusion.2
  162.3 4.4 fusion.80
  166.8 1.9 broadcast_multiply_fusion.2
  168.7 18.2 %copy_bitcast_fusion.11 = (f32[96,16384]{1,0:T(8,128)}, f32[96,16384]{1,0:T(8,128)}) fusion(f32[12,8,128,128]{3,2,1,0:T(8,128)} %bitcast.160, f32[12,8,128,128]{3,2,1,0:T(8,128)S(1)} %bitcast.159), kind=kLoop, calls=%fused_computation.6.clone.1 | loop fusion | bytes 25165824 | tf_op jit(solution)/shard_map/while/body/eval_jaxpr/reshape | solution.py:76
  186.9 14.6 %convolution_add_fusion.2 = f32[48,32768]{1,0:T(8,128)} fusion(f32[96,16384]{1,0:T(8,128)} %get-tuple-element.181, f32[96,16384]{1,0:T(8,128)} %get-tuple-element.182, f32[48,32768]{1,0:T(8,128)} %get-tuple-element.195, pred[]{:T(512)S(6)} %compare.3, s32[96]{0:T(128)S(1)} %eq.39), kind=kOutput, calls=%fused_computation.2.clone.1 | convolution fusion | flops 1818235392 | bytes 25166208 | tf_op jit(solution)/shard_map/while/body/eval_jaxpr/dot_general | solution.py:78
  205.9 2.0 fusion.78
  209.4 3.2 multiply_convert_fusion.2
  214.4 4.4 fusion.80
  218.9 1.9 broadcast_multiply_fusion.2
  220.8 18.2 %copy_bitcast_fusion.11 = (f32[96,16384]{1,0:T(8,128)}, f32[96,16384]{1,0:T(8,128)}) fusion(f32[12,8,128,128]{3,2,1,0:T(8,128)} %bitcast.160, f32[12,8,128,128]{3,2,1,0:T(8,128)S(1)} %bitcast.159), kind=kLoop, calls=%fused_computation.6.clone.1 | loop fusion | bytes 25165824 | tf_op jit(solution)/shard_map/while/body/eval_jaxpr/reshape | solution.py:76
  239.0 15.5 %convolution_add_fusion.2 = f32[48,32768]{1,0:T(8,128)} fusion(f32[96,16384]{1,0:T(8,128)} %get-tuple-element.181, f32[96,16384]{1,0:T(8,128)} %get-tuple-element.182, f32[48,32768]{1,0:T(8,128)} %get-tuple-element.195, pred[]{:T(512)S(6)} %compare.3, s32[96]{0:T(128)S(1)} %eq.39), kind=kOutput, calls=%fused_computation.2.clone.1 | convolution fusion | flops 1818235392 | bytes 25166208 | tf_op jit(solution)/shard_map/while/body/eval_jaxpr/dot_general | solution.py:78
  258.9 2.0 fusion.78
  262.5 3.2 multiply_convert_fusion.2
  267.5 4.4 fusion.80
  271.9 1.9 broadcast_multiply_fusion.2
  273.9 18.2 %copy_bitcast_fusion.11 = (f32[96,16384]{1,0:T(8,128)}, f32[96,16384]{1,0:T(8,128)}) fusion(f32[12,8,128,128]{3,2,1,0:T(8,128)} %bitcast.160, f32[12,8,128,128]{3,2,1,0:T(8,128)S(1)} %bitcast.159), kind=kLoop, calls=%fused_computation.6.clone.1 | loop fusion | bytes 25165824 | tf_op jit(solution)/shard_map/while/body/eval_jaxpr/reshape | solution.py:76
  292.1 15.5 %convolution_add_fusion.2 = f32[48,32768]{1,0:T(8,128)} fusion(f32[96,16384]{1,0:T(8,128)} %get-tuple-element.181, f32[96,16384]{1,0:T(8,128)} %get-tuple-element.182, f32[48,32768]{1,0:T(8,128)} %get-tuple-element.195, pred[]{:T(512)S(6)} %compare.3, s32[96]{0:T(128)S(1)} %eq.39), kind=kOutput, calls=%fused_computation.2.clone.1 | convolution fusion | flops 1818235392 | bytes 25166208 | tf_op jit(solution)/shard_map/while/body/eval_jaxpr/dot_general | solution.py:78
  312.0 2.0 fusion.78
  315.6 3.2 multiply_convert_fusion.2
  320.6 4.4 fusion.80
  326.9 18.2 %copy_bitcast_fusion.11 = (f32[96,16384]{1,0:T(8,128)}, f32[96,16384]{1,0:T(8,128)}) fusion(f32[12,8,128,128]{3,2,1,0:T(8,128)} %bitcast.160, f32[12,8,128,128]{3,2,1,0:T(8,128)S(1)} %bitcast.159), kind=kLoop, calls=%fused_computation.6.clone.1 | loop fusion | bytes 25165824 | tf_op jit(solution)/shard_map/while/body/eval_jaxpr/reshape | solution.py:76
  345.1 15.5 %convolution_add_fusion.2 = f32[48,32768]{1,0:T(8,128)} fusion(f32[96,16384]{1,0:T(8,128)} %get-tuple-element.181, f32[96,16384]{1,0:T(8,128)} %get-tuple-element.182, f32[48,32768]{1,0:T(8,128)} %get-tuple-element.195, pred[]{:T(512)S(6)} %compare.3, s32[96]{0:T(128)S(1)} %eq.39), kind=kOutput, calls=%fused_computation.2.clone.1 | convolution fusion | flops 1818235392 | bytes 25166208 | tf_op jit(solution)/shard_map/while/body/eval_jaxpr/dot_general | solution.py:78
  365.1 2.0 fusion.78
  368.6 3.2 multiply_convert_fusion.2
  373.6 4.4 fusion.80
  378.1 1.9 broadcast_multiply_fusion.2
  380.0 18.2 %copy_bitcast_fusion.11 = (f32[96,16384]{1,0:T(8,128)}, f32[96,16384]{1,0:T(8,128)}) fusion(f32[12,8,128,128]{3,2,1,0:T(8,128)} %bitcast.160, f32[12,8,128,128]{3,2,1,0:T(8,128)S(1)} %bitcast.159), kind=kLoop, calls=%fused_computation.6.clone.1 | loop fusion | bytes 25165824 | tf_op jit(solution)/shard_map/while/body/eval_jaxpr/reshape | solution.py:76
  398.2 15.5 %convolution_add_fusion.2 = f32[48,32768]{1,0:T(8,128)} fusion(f32[96,16384]{1,0:T(8,128)} %get-tuple-element.181, f32[96,16384]{1,0:T(8,128)} %get-tuple-element.182, f32[48,32768]{1,0:T(8,128)} %get-tuple-element.195, pred[]{:T(512)S(6)} %compare.3, s32[96]{0:T(128)S(1)} %eq.39), kind=kOutput, calls=%fused_computation.2.clone.1 | convolution fusion | flops 1818235392 | bytes 25166208 | tf_op jit(solution)/shard_map/while/body/eval_jaxpr/dot_general | solution.py:78
  418.2 2.0 fusion.78
  421.7 3.2 multiply_convert_fusion.2
  426.7 4.4 fusion.80
  431.2 1.9 broadcast_multiply_fusion.2
  433.1 18.2 %copy_bitcast_fusion.11 = (f32[96,16384]{1,0:T(8,128)}, f32[96,16384]{1,0:T(8,128)}) fusion(f32[12,8,128,128]{3,2,1,0:T(8,128)} %bitcast.160, f32[12,8,128,128]{3,2,1,0:T(8,128)S(1)} %bitcast.159), kind=kLoop, calls=%fused_computation.6.clone.1 | loop fusion | bytes 25165824 | tf_op jit(solution)/shard_map/while/body/eval_jaxpr/reshape | solution.py:76
  451.3 15.5 %convolution_add_fusion.2 = f32[48,32768]{1,0:T(8,128)} fusion(f32[96,16384]{1,0:T(8,128)} %get-tuple-element.181, f32[96,16384]{1,0:T(8,128)} %get-tuple-element.182, f32[48,32768]{1,0:T(8,128)} %get-tuple-element.195, pred[]{:T(512)S(6)} %compare.3, s32[96]{0:T(128)S(1)} %eq.39), kind=kOutput, calls=%fused_computation.2.clone.1 | convolution fusion | flops 1818235392 | bytes 25166208 | tf_op jit(solution)/shard_map/while/body/eval_jaxpr/dot_general | solution.py:78
  466.8 4.0 all-to-all-start.5
  470.8 3.1 convert.5
  475.3 3.7 convert_element_type.41
  479.0 15.7 %all-to-all-done.5 = bf16[32,192,128]{2,1,0:T(8,128)(2,1)S(1)} async-done(((bf16[32,192,128]{2,1,0:T(8,128)(2,1)}), bf16[32,192,128]{2,1,0:T(8,128)(2,1)S(1)}, u32[]{:S(2)}, u32[]{:S(2)}) %all-to-all-start.5) | async-done | bytes 1572896 | tf_op jit(solution)/shard_map/all_to_all | solution.py:122
  494.7 4.7 all-to-all-start.7
  499.4 2.1 convert_element_type.40
  501.5 21.8 %all-to-all-done.7 = bf16[32,192,128]{2,1,0:T(8,128)(2,1)} async-done(((bf16[32,192,128]{2,1,0:T(8,128)(2,1)}), bf16[32,192,128]{2,1,0:T(8,128)(2,1)}, u32[]{:S(2)}, u32[]{:S(2)}) %all-to-all-start.7) | async-done | bytes 1572896 | tf_op jit(solution)/shard_map/all_to_all | solution.py:124
  523.4 4.7 all-to-all-start.6
  529.5 2.8 copy_bitcast_fusion.2
  532.3 19.7 %all-to-all-done.6 = bf16[32,192,128]{2,1,0:T(8,128)(2,1)} async-done(((bf16[32,192,128]{2,1,0:T(8,128)(2,1)}), bf16[32,192,128]{2,1,0:T(8,128)(2,1)}, u32[]{:S(2)}, u32[]{:S(2)}) %all-to-all-start.6) | async-done | bytes 1572896 | tf_op jit(solution)/shard_map/all_to_all | solution.py:123
  552.0 2.8 copy_bitcast_fusion.3
  (120 shorter events, 58.5 us)
Async XLA Ops:
  0.6 1.4 copy-start
  3.6 7.5 %copy-start.8 = (bf16[192,4096]{1,0:T(8,128)(2,1)S(1)}, bf16[192,4096]{1,0:T(8,128)(2,1)}, u32[]{:S(2)}) copy-start(bf16[192,4096]{1,0:T(8,128)(2,1)} %param.11) | copy-start | bytes 4718596
  3.6 31.5 %all-to-all-start.1 = ((bf16[192,32,128]{2,0,1:T(8,128)(2,1)}), bf16[192,32,128]{2,0,1:T(8,128)(2,1)S(1)}, u32[]{:S(2)}, u32[]{:S(2)}) async-start(bf16[192,32,128]{2,0,1:T(8,128)(2,1)} %copy_bitcast_fusion.8), calls=%async_computation.1 | async-start | bytes 3145728 | tf_op jit(solution)/shard_map/all_to_all | solution.py:101
  35.1 27.9 %all-to-all-start.2 = ((bf16[192,32,128]{2,0,1:T(8,128)(2,1)}), bf16[192,32,128]{2,0,1:T(8,128)(2,1)S(1)}, u32[]{:S(2)}, u32[]{:S(2)}) async-start(bf16[192,32,128]{2,0,1:T(8,128)(2,1)} %copy_bitcast_fusion.7), calls=%async_computation.2 | async-start | bytes 3145728 | tf_op jit(solution)/shard_map/all_to_all | solution.py:102
  63.0 1.1 copy-start.6
  64.2 27.9 %all-to-all-start.3 = ((bf16[192,32,128]{2,0,1:T(8,128)(2,1)}), bf16[192,32,128]{2,0,1:T(8,128)(2,1)S(1)}, u32[]{:S(2)}, u32[]{:S(2)}) async-start(bf16[192,32,128]{2,0,1:T(8,128)(2,1)} %copy_bitcast_fusion.6), calls=%async_computation.3 | async-start | bytes 3145728 | tf_op jit(solution)/shard_map/all_to_all | solution.py:103
  68.1 29.2 %copy-start.10 = (s32[1,48]{1,0:T(1,128)S(1)}, s32[1,48]{1,0:T(1,128)}, u32[]{:S(2)}) copy-start(s32[1,48]{1,0:T(1,128)} %param.15) | copy-start | bytes 580
  68.2 29.9 %copy-start.9 = (s32[1,48,12]{1,0,2:T(1,128)S(1)}, s32[1,48,12]{1,0,2:T(1,128)}, u32[]{:S(2)}) copy-start(s32[1,48,12]{1,0,2:T(1,128)} %param.14) | copy-start | bytes 6916
  92.1 9.1 %copy-start.4 = (bf16[192,32,128]{2,0,1:T(8,128)(2,1)}, bf16[192,32,128]{2,0,1:T(8,128)(2,1)S(1)}, u32[]{:S(2)}) copy-start(bf16[192,32,128]{2,0,1:T(8,128)(2,1)S(1)} %all-to-all-done.3) | copy-start | bytes 4718596
  92.1 28.6 %all-to-all-start.4 = ((bf16[192,32,128]{2,0,1:T(8,128)(2,1)}), bf16[192,32,128]{2,0,1:T(8,128)(2,1)}, u32[]{:S(2)}, u32[]{:S(2)}) async-start(bf16[192,32,128]{2,0,1:T(8,128)(2,1)} %copy_bitcast_fusion.5), calls=%async_computation.4 | async-start | bytes 3145728 | tf_op jit(solution)/shard_map/all_to_all | solution.py:104
  101.1 2.0 copy-start.7
  120.7 28.6 %all-to-all-start = ((bf16[192,32,128]{2,0,1:T(8,128)(2,1)}), bf16[192,32,128]{2,0,1:T(8,128)(2,1)}, u32[]{:S(2)}, u32[]{:S(2)}) async-start(bf16[192,32,128]{2,0,1:T(8,128)(2,1)} %copy_bitcast_fusion.9), calls=%async_computation | async-start | bytes 3145728 | tf_op jit(solution)/shard_map/all_to_all | solution.py:100
  125.4 2.4 copy-start.5
  149.3 2.0 copy-start.2
  186.9 14.6 %copy-start.3 = (bf16[48,32768]{1,0:T(8,128)(2,1)S(1)}, bf16[48,32768]{1,0:T(8,128)(2,1)}, u32[]{:S(2)}) copy-start(bf16[48,32768]{1,0:T(8,128)(2,1)} %copy-done.2) | copy-start | bytes 9437188 | tf_op jit(solution)/shard_map/while
  201.5 2.0 copy-start.2
  239.0 15.5 %copy-start.3 = (bf16[48,32768]{1,0:T(8,128)(2,1)S(1)}, bf16[48,32768]{1,0:T(8,128)(2,1)}, u32[]{:S(2)}) copy-start(bf16[48,32768]{1,0:T(8,128)(2,1)} %copy-done.2) | copy-start | bytes 9437188 | tf_op jit(solution)/shard_map/while
  254.5 2.0 copy-start.2
  292.1 15.5 %copy-start.3 = (bf16[48,32768]{1,0:T(8,128)(2,1)S(1)}, bf16[48,32768]{1,0:T(8,128)(2,1)}, u32[]{:S(2)}) copy-start(bf16[48,32768]{1,0:T(8,128)(2,1)} %copy-done.2) | copy-start | bytes 9437188 | tf_op jit(solution)/shard_map/while
  307.6 2.0 copy-start.2
  345.1 15.5 %copy-start.3 = (bf16[48,32768]{1,0:T(8,128)(2,1)S(1)}, bf16[48,32768]{1,0:T(8,128)(2,1)}, u32[]{:S(2)}) copy-start(bf16[48,32768]{1,0:T(8,128)(2,1)} %copy-done.2) | copy-start | bytes 9437188 | tf_op jit(solution)/shard_map/while
  360.7 2.0 copy-start.2
  398.2 15.5 %copy-start.3 = (bf16[48,32768]{1,0:T(8,128)(2,1)S(1)}, bf16[48,32768]{1,0:T(8,128)(2,1)}, u32[]{:S(2)}) copy-start(bf16[48,32768]{1,0:T(8,128)(2,1)} %copy-done.2) | copy-start | bytes 9437188 | tf_op jit(solution)/shard_map/while
  413.7 2.0 copy-start.2
  451.3 15.5 %copy-start.3 = (bf16[48,32768]{1,0:T(8,128)(2,1)S(1)}, bf16[48,32768]{1,0:T(8,128)(2,1)}, u32[]{:S(2)}) copy-start(bf16[48,32768]{1,0:T(8,128)(2,1)} %copy-done.2) | copy-start | bytes 9437188 | tf_op jit(solution)/shard_map/while
  466.8 27.9 %all-to-all-start.5 = ((bf16[32,192,128]{2,1,0:T(8,128)(2,1)}), bf16[32,192,128]{2,1,0:T(8,128)(2,1)S(1)}, u32[]{:S(2)}, u32[]{:S(2)}) async-start(bf16[32,192,128]{2,1,0:T(8,128)(2,1)} %bitcast.165), calls=%async_computation.5 | async-start | bytes 3145728 | tf_op jit(solution)/shard_map/all_to_all | solution.py:122
  494.7 28.6 %all-to-all-start.7 = ((bf16[32,192,128]{2,1,0:T(8,128)(2,1)}), bf16[32,192,128]{2,1,0:T(8,128)(2,1)}, u32[]{:S(2)}, u32[]{:S(2)}) async-start(bf16[32,192,128]{2,1,0:T(8,128)(2,1)} %convert_element_type.41), calls=%async_computation.7 | async-start | bytes 3145728 | tf_op jit(solution)/shard_map/all_to_all | solution.py:124
  523.4 28.6 %all-to-all-start.6 = ((bf16[32,192,128]{2,1,0:T(8,128)(2,1)}), bf16[32,192,128]{2,1,0:T(8,128)(2,1)}, u32[]{:S(2)}, u32[]{:S(2)}) async-start(bf16[32,192,128]{2,1,0:T(8,128)(2,1)} %convert_element_type.40), calls=%async_computation.6 | async-start | bytes 3145728 | tf_op jit(solution)/shard_map/all_to_all | solution.py:123
  528.1 26.7 %copy-start.1 = (bf16[192,4096]{1,0:T(8,128)(2,1)S(1)}, bf16[192,4096]{1,0:T(8,128)(2,1)}, u32[]{:S(2)}) copy-start(bf16[192,4096]{1,0:T(8,128)(2,1)} %param.10) | copy-start | bytes 4718596
where the time goes:
time: 557 us; the launch traced here: 555 us
  matrix products  183 us (33%)
  local copies, waits for them, and re-layouts  158 us (28%)
  waiting for transfers between devices  156 us (28%)
  starting transfers between devices  38.3 us (7%)
  other arithmetic  18.3 us (3%)
    reshape x6, local copies, waits for them, and re-layouts, one_step(): value_part.reshape(-1, tile_width)  109 us
    dot_general x6, matrix products, one_step(): lax.dot_general(selector.astype(jnp.float32), parts_both, (((0,), (0,)),...  92.2 us
    dot_general x6, matrix products, one_step(): jnp.einsum('gqkj,gqd->gkjd', probs_low, grad_tile, preferred_element_type...  26.6 us
    all_to_all x1, waiting for transfers between devices, per_device(): lax.all_to_all(key_vectors, 'head', split_axis=1, concat_axis=0, tiled=True)  22.3 us
    all_to_all x1, waiting for transfers between devices, per_device(): lax.all_to_all(value_list, 'head', split_axis=0, concat_axis=1, tiled=True)  21.8 us
    all_to_all x1, waiting for transfers between devices, per_device(): lax.all_to_all(values, 'head', split_axis=1, concat_axis=0, tiled=True)  20.9 us
    all_to_all x1, waiting for transfers between devices, per_device(): lax.all_to_all(out_grad, 'head', split_axis=1, concat_axis=0, tiled=True)  20.8 us
    all_to_all x1, waiting for transfers between devices, per_device(): lax.all_to_all(key_list, 'head', split_axis=0, concat_axis=1, tiled=True)  19.7 us
  transfers between devices with their start and end apart: 8, of which 8 were waited for; matrix products, arithmetic and copies ran while one was open for 6% of the time, Pallas kernels for 0%

commit v1 on v0

v1 whole, which is shorter than its diff:
```python
import functools

import jax
import jax.numpy as jnp
from jax import lax
from jax.experimental import pallas as pl
from jax.experimental.pallas import tpu as pltpu
from jax.sharding import PartitionSpec as P

HD = 128
BLK = 128
SHARDS = 32
ROWS = 192
TOKENS = SHARDS * ROWS
NB = TOKENS // BLK
KMAX = 12
MAXPAIR = KMAX // 2
COLS = 4
SCALE = HD**-0.5
EXP2_SCALE = SCALE * 1.4426950408889634
NEG = -1e30
f32 = jnp.float32
bf16 = jnp.bfloat16

VMEM_SPEC = pl.BlockSpec(memory_space=pltpu.VMEM)
SMEM_SPEC = pl.BlockSpec(memory_space=pltpu.SMEM)


def dot(a, b):
    return lax.dot_general(a, b, (((1,), (0,)), ((), ())), preferred_element_type=f32)


def rows(ref, i):
    return ref[pl.ds(pl.multiple_of(i * BLK, BLK), BLK), :]


def wide(a, b):
    return jnp.concatenate([a, b], axis=1)


def diagonal(ref, x):
    ref[0:BLK, 0:BLK] = x
    ref[BLK : 2 * BLK, BLK : 2 * BLK] = x


def pack_kernel(q_ref, k_ref, g_ref, x_ref):
    for c in range(COLS):
        for i, ref in enumerate((q_ref, k_ref, g_ref)):
            x_ref[c, i] = ref[:, c * HD : (c + 1) * HD]


def pack(q, k, g):
    block = pl.BlockSpec((ROWS, COLS * HD), lambda h: (0, h))
    return pl.pallas_call(
        pack_kernel,
        grid=(SHARDS // COLS,),
        in_specs=[block] * 3,
        out_specs=pl.BlockSpec((COLS, 3, ROWS, HD), lambda h: (h, 0, 0, 0)),
        out_shape=jax.ShapeDtypeStruct((SHARDS, 3, ROWS, HD), bf16),
        cost_estimate=pl.CostEstimate(flops=0, bytes_accessed=9437184, transcendentals=0),
        name="pack_qkg",
    )(q, k, g)


def pack_values_kernel(parity_ref, v_ref, g_ref, o_ref, x_ref):
    odd = parity_ref[0] == 1
    gap = jnp.zeros((64, HD), f32)
    ones = jnp.ones((8, HD), bf16)
    sub = lax.broadcasted_iota(jnp.int32, (8, HD), 0)
    contract = (((1,), (1,)), ((), ()))
    for c in range(COLS):
        cols = slice(c * HD, (c + 1) * HD)
        x_ref[c, 0:ROWS] = v_ref[:, cols]
        prod = g_ref[:, cols].astype(f32) * o_ref[:, cols].astype(f32)
        prod = jnp.where(
            odd, jnp.concatenate([gap, prod], axis=0), jnp.concatenate([prod, gap], axis=0)
        )
        high = prod.astype(bf16)
        low = (prod - high.astype(f32)).astype(bf16)
        terms = lax.dot_general(ones, high, contract, preferred_element_type=f32)
        terms += lax.dot_general(ones, low, contract, preferred_element_type=f32)
        out = jnp.zeros((8, HD), f32)
        rest = terms
        for part in range(3):
            piece = rest.astype(bf16).astype(f32)
            rest = rest - piece
            out = jnp.where(sub == 2 * part, piece[:, :HD], out)
            out = jnp.where(sub == 2 * part + 1, piece[:, HD:], out)
        x_ref[c, ROWS : ROWS + 8] = out.astype(bf16)


def pack_values(parity, v, g, o):
    block = pl.BlockSpec((ROWS, COLS * HD), lambda h: (0, h))
    return pl.pallas_call(
        pack_values_kernel,
        grid=(SHARDS // COLS,),
        in_specs=[SMEM_SPEC] + [block] * 3,
        out_specs=pl.BlockSpec((COLS, ROWS + 8, HD), lambda h: (h, 0, 0)),
        out_shape=jax.ShapeDtypeStruct((SHARDS, ROWS + 8, HD), bf16),
        cost_estimate=pl.CostEstimate(flops=0, bytes_accessed=6291456, transcendentals=0),
        name="pack_v",
    )(parity, v, g, o)


def unpack_kernel(*refs):
    x_ref, outs = refs[0], refs[1:]
    for c in range(COLS):
        for i, ref in enumerate(outs):
            ref[:, c * HD : (c + 1) * HD] = x_ref[c, i]


def unpack(x):
    count = x.shape[1]
    return pl.pallas_call(
        unpack_kernel,
        grid=(SHARDS // COLS,),
        in_specs=[pl.BlockSpec((COLS, count, ROWS, HD), lambda h: (h, 0, 0, 0))],
        out_specs=[pl.BlockSpec((ROWS, COLS * HD), lambda h: (0, h))] * count,
        out_shape=[jax.ShapeDtypeStruct((ROWS, SHARDS * HD), bf16)] * count,
        cost_estimate=pl.CostEstimate(
            flops=0, bytes_accessed=count * 3145728, transcendentals=0
        ),
        compiler_params=pltpu.CompilerParams(vmem_limit_bytes=16 << 20),
        name="unpack",
    )(x)


def store_block(ref, part, block, value):
    for half in range(2):
        piece = 2 * block + half
        shard = piece // 3
        start = pl.multiple_of((piece - 3 * shard) * 64, 64)
        ref[shard, part, pl.ds(start, 64), :] = value[64 * half : 64 * half + 64]


def slot_pair(blocks, a, p, last, full):
    i0 = blocks[a, 2 * p]
    i1 = blocks[a, 2 * p + 1]
    if not last:
        return i0, i1, i1
    return i0, jnp.where(full, i1, i0), jnp.where(full, i1, NB)


def dead_half(full):
    lane = lax.broadcasted_iota(jnp.int32, (1, 2 * BLK), 1)
    return jnp.logical_and(lane >= BLK, jnp.logical_not(full))


def first_kernel(blocks, counts, q_ref, k_ref, g_ref, dv_ref, lse_ref, acc, st, wq, wg):
    q = q_ref.reshape(TOKENS, HD)
    k = k_ref.reshape(TOKENS, HD)
    g = g_ref.reshape(TOKENS, HD)
    acc[...] = jnp.zeros_like(acc)
    wq[...] = jnp.zeros_like(wq)
    wg[...] = jnp.zeros_like(wg)

    def work(a, n, pairs):
        full = n == 2 * pairs
        top = None
        ids = []
        for p in range(pairs):
            last = p == pairs - 1
            i0, i1, j1 = slot_pair(blocks, a, p, last, full)
            ids.append((i0, j1))
            s = dot(wide(rows(k, i0), rows(k, i1)), wq[...])
            if last:
                s = jnp.where(dead_half(full), NEG, s)
            st[p] = s
            here = jnp.max(s, axis=0, keepdims=True)
            top = here if top is None else jnp.maximum(top, here)
        top = jnp.maximum(top[:, :BLK], top[:, BLK:]) * EXP2_SCALE
        top2 = wide(top, top)
        total = None
        for p in range(pairs):
            e = jnp.exp2(st[p] * EXP2_SCALE - top2)
            st[p] = e
            here = jnp.sum(e, axis=0, keepdims=True)
            total = here if total is None else total + here
        total = total[:, :BLK] + total[:, BLK:]
        lse_ref[a] = top + jnp.log2(total)
        inverse = 1.0 / total
        inverse2 = wide(inverse, inverse)
        for p in range(pairs):
            dv = dot((st[p] * inverse2).astype(bf16), wg[...])
            i0, j1 = ids[p]
            b0 = acc[i0] + dv[:, :BLK]
            b1 = acc[j1] + dv[:, BLK:]
            acc[i0] = b0
            acc[j1] = b1

    def body(a, carry):
        n = counts[0, a]
        diagonal(wq, rows(q, a).T)
        diagonal(wg, rows(g, a))
        for pairs in range(1, MAXPAIR + 1):
            pl.when((n + 1) // 2 == pairs)(functools.partial(work, a, n, pairs))
        return carry

    lax.fori_loop(0, NB, body, 0)

    def finish(b, carry):
        store_block(dv_ref, 0, b, acc[b].astype(bf16))
        return carry

    lax.fori_loop(0, NB, finish, 0)


def second_kernel(
    blocks, counts, q_ref, k_ref, g_ref, v_ref, t_ref, lse_ref, out_ref, acc, kt, terms, wq, wg, wn
):
    q = q_ref.reshape(TOKENS, HD)
    k = k_ref.reshape(TOKENS, HD)
    g = g_ref.reshape(TOKENS, HD)
    v = v_ref.reshape(TOKENS, HD)
    acc[...] = jnp.zeros_like(acc)
    wq[...] = jnp.zeros_like(wq)
    wg[...] = jnp.zeros_like(wg)
    wn[...] = jnp.zeros_like(wn)

    def prepare(t, carry):
        a = t_ref[2 * t].astype(f32)
        b = t_ref[2 * t + 1].astype(f32)
        a0 = a[0:1] + a[2:3] + a[4:5]
        a1 = a[1:2] + a[3:4] + a[5:6]
        b0 = b[0:1] + b[2:3] + b[4:5]
        b1 = b[1:2] + b[3:4] + b[5:6]
        terms[3 * t] = a0
        terms[3 * t + 1] = a1 + b0
        terms[3 * t + 2] = b1
        for r in range(3):
            kt[3 * t + r] = rows(k, 3 * t + r).T
        return carry

    lax.fori_loop(0, NB // 3, prepare, 0)

    def work(a, n, pairs):
        full = n == 2 * pairs
        lse = wide(lse_ref[a], lse_ref[a])
        term = wide(terms[a], terms[a])
        dq = None
        for p in range(pairs):
            last = p == pairs - 1
            i0, i1, j1 = slot_pair(blocks, a, p, last, full)
            s = dot(wide(rows(k, i0), rows(k, i1)), wq[...])
            dp = dot(wide(rows(v, i0), rows(v, i1)), wg[...])
            ds = jnp.exp2(s * EXP2_SCALE - lse) * (dp - term)
            if last:
                ds = jnp.where(dead_half(full), 0.0, ds)
            ds = ds.astype(bf16)
            dk = dot(ds, wn[...])
            b0 = acc[i0] + dk[:, :BLK]
            b1 = acc[j1] + dk[:, BLK:]
            acc[i0] = b0
            acc[j1] = b1
            part = dot(
                wide(kt[i0], kt[i1]), jnp.concatenate([ds[:, :BLK], ds[:, BLK:]], axis=0)
            )
            dq = part if dq is None else dq + part
        store_block(out_ref, 0, a, (dq.T * SCALE).astype(bf16))

    def body(a, carry):
        n = counts[0, a]
        qb = rows(q, a)
        diagonal(wq, qb.T)
        diagonal(wn, qb)
        diagonal(wg, rows(g, a).T)
        for pairs in range(1, MAXPAIR + 1):
            pl.when((n + 1) // 2 == pairs)(functools.partial(work, a, n, pairs))
        return carry

    lax.fori_loop(0, NB, body, 0)

    def finish(b, carry):
        store_block(out_ref, 1, b, (acc[b] * SCALE).astype(bf16))
        return carry

    lax.fori_loop(0, NB, finish, 0)


def part_specs(count):
    return [
        pl.BlockSpec((SHARDS, None, ROWS, HD), functools.partial(lambda i, _: (0, i, 0, 0), i))
        for i in range(count)
    ]


def first_phase(blocks, counts, x):
    return pl.pallas_call(
        first_kernel,
        grid=(1,),
        in_specs=[SMEM_SPEC, SMEM_SPEC] + part_specs(3),
        out_specs=[VMEM_SPEC] * 2,
        out_shape=[
            jax.ShapeDtypeStruct((SHARDS, 1, ROWS, HD), bf16),
            jax.ShapeDtypeStruct((NB, 1, BLK), f32),
        ],
        scratch_shapes=[
            pltpu.VMEM((NB + 1, BLK, HD), f32),
            pltpu.VMEM((MAXPAIR, BLK, 2 * BLK), f32),
            pltpu.VMEM((2 * BLK, 2 * BLK), bf16),
            pltpu.VMEM((2 * BLK, 2 * BLK), bf16),
        ],
        compiler_params=pltpu.CompilerParams(vmem_limit_bytes=40 << 20),
        cost_estimate=pl.CostEstimate(
            flops=20_000_000_000, bytes_accessed=6291456, transcendentals=5_000_000
        ),
        name="softmax_and_values",
    )(blocks, counts, x, x, x)


def second_phase(blocks, counts, x, v, lse):
    return pl.pallas_call(
        second_kernel,
        grid=(1,),
        in_specs=[SMEM_SPEC, SMEM_SPEC]
        + part_specs(3)
        + [
            pl.BlockSpec((SHARDS, ROWS, HD), lambda _: (0, 0, 0)),
            pl.BlockSpec((SHARDS, 8, HD), lambda _: (0, ROWS // 8, 0)),
            VMEM_SPEC,
        ],
        out_specs=VMEM_SPEC,
        out_shape=jax.ShapeDtypeStruct((SHARDS, 2, ROWS, HD), bf16),
        scratch_shapes=[
            pltpu.VMEM((NB + 1, BLK, HD), f32),
            pltpu.VMEM((NB, HD, BLK), bf16),
            pltpu.VMEM((NB, 1, BLK), f32),
        ]
        + [pltpu.VMEM((2 * BLK, 2 * BLK), bf16)] * 3,
        compiler_params=pltpu.CompilerParams(vmem_limit_bytes=40 << 20),
        cost_estimate=pl.CostEstimate(
            flops=20_000_000_000, bytes_accessed=9437184, transcendentals=5_000_000
        ),
        name="scores_and_gradients",
    )(blocks, counts, x, x, x, v, v, lse)


def exchange(x):
    return lax.all_to_all(x, "head", split_axis=0, concat_axis=0, tiled=True)


def per_device(queries, key_vectors, values, out_grad, output, key_blocks, block_count):
    parity = (lax.axis_index("head") % 2).astype(jnp.int32).reshape(1)
    blocks = key_blocks[0]
    x = exchange(pack(queries, key_vectors, out_grad))
    v = exchange(pack_values(parity, values, out_grad, output))
    dv, lse = first_phase(blocks, block_count, x)
    (value_grad,) = unpack(exchange(dv))
    query_grad, key_grad = unpack(exchange(second_phase(blocks, block_count, x, v, lse)))
    return query_grad, key_grad, value_grad


def solution(mesh):
    token = P(("dp", "head"), None)
    return jax.shard_map(
        per_device,
        mesh=mesh,
        in_specs=(token,) * 5 + (P(("dp", "head"), None, None), token),
        out_specs=(token,) * 3,
        check_vma=False,
    )
```

time: 557 us -> 237 us (0.43)
  matrix products: 183 us -> 0 us
  local copies, waits for them, and re-layouts: 158 us -> 5.42 us
  Pallas kernels: 0 us -> 87.1 us
  waiting for transfers between devices: 156 us -> 89.9 us
  other arithmetic: 18.3 us -> 0 us
  starting transfers between devices: 38.3 us -> 50.9 us
    dot_general x42 -> x0, matrix products: 183 us -> none  [the longest x6 92.2 us: one_step(): lax.dot_general(selector.astype(jnp.float32), parts_both, (((0,), (0,)),...]
    reshape x8 -> x0, local copies, waits for them, and re-layouts: 113 us -> none  [the longest x6 109 us: one_step(): value_part.reshape(-1, tile_width)]
    pallas_call x0 -> x6, Pallas kernels: none -> 87.1 us  [the longest x1 37.1 us: second_phase(): pl.pallas_call(second_kernel, grid=(1,), in_specs=[SMEM_SPEC, SMEM_SPEC]...]
    all_to_all x8 -> x4, waiting for transfers between devices: 156 us -> 89.9 us  [exchange(): return lax.all_to_all(x, 'head', split_axis=0, concat_axis=0, tiled=True)]
    all_to_all x8 -> x0, local copies, waits for them, and re-layouts: 19.2 us -> none  [the longest x1 3.1 us: per_device(): lax.all_to_all(output, 'head', split_axis=1, concat_axis=0, tiled=True)]
    while x42 -> x0, local copies, waits for them, and re-layouts: 14.3 us -> none
    all_to_all x8 -> x4, starting transfers between devices: 38.3 us -> 50.9 us  [exchange(): return lax.all_to_all(x, 'head', split_axis=0, concat_axis=0, tiled=True)]
    reduce_sum x7 -> x0, other arithmetic: 11.9 us -> none  [the longest x6 9.34 us: one_step(): probs = weights / jnp.sum(weights, axis=(2, 3), keepdims=True)]
  transfers between devices with their start and end apart: 8 -> 4, of which waited for: 8 -> 2; matrix products, arithmetic and copies ran while one was open for 6% -> 0% of each run, Pallas kernels for 0% -> 33%
where the time goes in v1:
time: 237 us; the launch traced here: 234 us
  waiting for transfers between devices  89.9 us (38%)
  Pallas kernels  87.1 us (37%)
  starting transfers between devices  50.9 us (21%)
  local copies, waits for them, and re-layouts  5.42 us (2%)
    all_to_all x4, waiting for transfers between devices, exchange(): return lax.all_to_all(x, 'head', split_axis=0, concat_axis=0, tiled=True)  89.9 us
    all_to_all x4, starting transfers between devices, exchange(): return lax.all_to_all(x, 'head', split_axis=0, concat_axis=0, tiled=True)  50.9 us
    pallas_call x1, Pallas kernels, second_phase(): pl.pallas_call(second_kernel, grid=(1,), in_specs=[SMEM_SPEC, SMEM_SPEC]...  37.1 us
    pallas_call x1, Pallas kernels, first_phase(): pl.pallas_call(first_kernel, grid=(1,), in_specs=[SMEM_SPEC, SMEM_SPEC] +...  29.3 us
    pallas_call x1, Pallas kernels, pack(): pl.pallas_call(pack_kernel, grid=(SHARDS // COLS,), in_specs=[block] * 3,...  7.22 us
    pallas_call x1, Pallas kernels, pack_values(): pl.pallas_call(pack_values_kernel, grid=(SHARDS // COLS,), in_specs=[SMEM...  7.18 us
    pallas_call x2, Pallas kernels, unpack(): pl.pallas_call(unpack_kernel, grid=(SHARDS // COLS,), in_specs=[pl.BlockS...  6.26 us
    unnamed x13, local copies, waits for them, and re-layouts  5.42 us
  transfers between devices with their start and end apart: 4, of which 2 were waited for; matrix products, arithmetic and copies ran while one was open for 0% of the time, Pallas kernels for 33%

profile of v1, /device:TPU:0, one launch (start us, length us, event | category | flops | bytes accessed | tf_op | source)
XLA Modules:
  0.0 234.0 jit_solution(10000253593000123855)
XLA Ops:
  0.6 7.2 %pack_qkg.1 = bf16[32,3,192,128]{3,2,1,0:T(8,128)(2,1)} custom-call(bf16[192,4096]{1,0:T(8,128)(2,1)} %q_ref.1, bf16[192,4096]{1,0:T(8,128)(2,1)} %k_ref.1, bf16[192,4096]{1,0:T(8,128)(2,1)} %g_ref.3), custom_call_target="tpu_custom_call" | custom-call | bytes 9437184 | tf_op jit(solution)/shard_map/pack_qkg/pallas_call | solution.py:54
  7.8 0.0 copy-start.5
  7.9 7.7 %all-to-all-start = ((bf16[32,3,192,128]{3,2,1,0:T(8,128)(2,1)}), bf16[32,3,192,128]{3,2,1,0:T(8,128)(2,1)}, u32[]{:S(2)}, u32[]{:S(2)}) async-start(bf16[32,3,192,128]{3,2,1,0:T(8,128)(2,1)} %pack_qkg.1), calls=%async_computation | async-start | bytes 9437184 | tf_op jit(solution)/shard_map/all_to_all | solution.py:339
  15.5 0.0 copy-done.5
  15.5 0.1 copy.10
  15.6 7.2 %pack_v.1 = bf16[32,200,128]{2,1,0:T(8,128)(2,1)} custom-call(s32[1]{0:T(128)} %bitcast.1.parity_ref, bf16[192,4096]{1,0:T(8,128)(2,1)} %v_ref.1, bf16[192,4096]{1,0:T(8,128)(2,1)} %g_ref.3, bf16[192,4096]{1,0:T(8,128)(2,1)} %o_ref.1), custom_call_target="tpu_custom_call" | custom-call | bytes 6291456 | tf_op jit(solution)/shard_map/pack_v/pallas_call | solution.py:94
  22.8 0.0 copy-start.4
  22.8 52.4 %all-to-all-done.q_ref.k_ref.g_ref = bf16[32,3,192,128]{3,2,1,0:T(8,128)(2,1)} async-done(((bf16[32,3,192,128]{3,2,1,0:T(8,128)(2,1)}), bf16[32,3,192,128]{3,2,1,0:T(8,128)(2,1)}, u32[]{:S(2)}, u32[]{:S(2)}) %all-to-all-start) | async-done | bytes 4718624 | tf_op jit(solution)/shard_map/all_to_all | solution.py:339
  75.3 4.0 %all-to-all-start.1 = ((bf16[32,200,128]{2,1,0:T(8,128)(2,1)}), bf16[32,200,128]{2,1,0:T(8,128)(2,1)S(1)}, u32[]{:S(2)}, u32[]{:S(2)}) async-start(bf16[32,200,128]{2,1,0:T(8,128)(2,1)} %pack_v.1), calls=%async_computation.1 | async-start | bytes 3276800 | tf_op jit(solution)/shard_map/all_to_all | solution.py:339
  79.2 0.0 copy-done.4
  79.2 29.3 %softmax_and_values.1 = (bf16[32,1,192,128]{3,2,1,0:T(8,128)(2,1)S(1)}, f32[48,1,128]{2,1,0:T(1,128)S(1)}) custom-call(s32[48,12]{1,0:T(8,128)S(1)} %bitcast.2, s32[1,48]{1,0:T(1,128)S(1)} %copy-done.4, bf16[32,3,192,128]{3,2,1,0:T(8,128)(2,1)} %all-to-all-done.q_ref.k_ref.g_ref, bf16[32,3,192,128]{3,2,1,0:T(8,128)(2,1)} %all-to-all-done.q_ref.k_ref.g_ref, ...), custom_call_target="tpu_custom_call" | custom-call | flops 20000000000 | bytes 6291456 | tf_op jit(solution)/shard_map/softmax_and_values/pallas_call | solution.py:288
  108.5 0.0 copy-start.3
  108.5 1.1 copy-done.3
  109.7 0.0 all-to-all-done.1.v_ref.t_ref
  109.7 13.1 %all-to-all-start.3 = ((bf16[32,1,192,128]{3,2,1,0:T(8,128)(2,1)}), bf16[32,1,192,128]{3,2,1,0:T(8,128)(2,1)S(1)}, u32[]{:S(2)}, u32[]{:S(2)}) async-start(bf16[32,1,192,128]{3,2,1,0:T(8,128)(2,1)} %copy-done.3), calls=%async_computation.3 | async-start | bytes 3145728 | tf_op jit(solution)/shard_map/all_to_all | solution.py:339
  122.8 37.1 %scores_and_gradients.1 = bf16[32,2,192,128]{3,2,1,0:T(8,128)(2,1)S(1)} custom-call(s32[48,12]{1,0:T(8,128)S(1)} %bitcast.3, s32[1,48]{1,0:T(1,128)S(1)} %copy-done.4, bf16[32,3,192,128]{3,2,1,0:T(8,128)(2,1)} %all-to-all-done.q_ref.k_ref.g_ref, bf16[32,3,192,128]{3,2,1,0:T(8,128)(2,1)} %all-to-all-done.q_ref.k_ref.g_ref, ...), custom_call_target="tpu_custom_call" | custom-call | flops 20000000000 | bytes 9437184 | tf_op jit(solution)/shard_map/scores_and_gradients/pallas_call | solution.py:312
  159.9 0.0 copy-start.2
  160.0 1.6 copy-done.2
  161.6 0.0 all-to-all-done.3.refs_0_
  161.6 0.0 copy-start
  161.6 1.1 copy-done
  162.7 26.1 %all-to-all-start.2 = ((bf16[32,2,192,128]{3,2,1,0:T(8,128)(2,1)}), bf16[32,2,192,128]{3,2,1,0:T(8,128)(2,1)S(1)}, u32[]{:S(2)}, u32[]{:S(2)}) async-start(bf16[32,2,192,128]{3,2,1,0:T(8,128)(2,1)} %copy-done.2), calls=%async_computation.2 | async-start | bytes 6291456 | tf_op jit(solution)/shard_map/all_to_all | solution.py:339
  188.9 0.0 copy-start.1
  188.9 1.4 copy-done.1
  190.3 2.9 %unpack.3 = bf16[192,4096]{1,0:T(8,128)(2,1)} custom-call(bf16[32,1,192,128]{3,2,1,0:T(8,128)(2,1)S(1)} %copy-done.1), custom_call_target="tpu_custom_call" | custom-call | bytes 3145728 | tf_op jit(solution)/shard_map/unpack/pallas_call | solution.py:114
  193.2 37.5 %all-to-all-done.2.refs_0_ = bf16[32,2,192,128]{3,2,1,0:T(8,128)(2,1)S(1)} async-done(((bf16[32,2,192,128]{3,2,1,0:T(8,128)(2,1)}), bf16[32,2,192,128]{3,2,1,0:T(8,128)(2,1)S(1)}, u32[]{:S(2)}, u32[]{:S(2)}) %all-to-all-start.2) | async-done | bytes 3145760 | tf_op jit(solution)/shard_map/all_to_all | solution.py:339
  230.6 3.4 %unpack.2 = (bf16[192,4096]{1,0:T(8,128)(2,1)}, bf16[192,4096]{1,0:T(8,128)(2,1)}) custom-call(bf16[32,2,192,128]{3,2,1,0:T(8,128)(2,1)S(1)} %all-to-all-done.2.refs_0_), custom_call_target="tpu_custom_call" | custom-call | bytes 6291456 | tf_op jit(solution)/shard_map/unpack/pallas_call | solution.py:114
Async XLA Ops:
  7.8 7.7 %copy-start.5 = (s32[1,48,12]{1,0,2:T(1,128)S(1)}, s32[1,48,12]{1,0,2:T(1,128)}, u32[]{:S(2)}) copy-start(s32[1,48,12]{1,0,2:T(1,128)} %param.12) | copy-start | bytes 6916
  7.9 67.4 %all-to-all-start = ((bf16[32,3,192,128]{3,2,1,0:T(8,128)(2,1)}), bf16[32,3,192,128]{3,2,1,0:T(8,128)(2,1)}, u32[]{:S(2)}, u32[]{:S(2)}) async-start(bf16[32,3,192,128]{3,2,1,0:T(8,128)(2,1)} %pack_qkg.1), calls=%async_computation | async-start | bytes 9437184 | tf_op jit(solution)/shard_map/all_to_all | solution.py:339
  22.8 56.4 %copy-start.4 = (s32[1,48]{1,0:T(1,128)S(1)}, s32[1,48]{1,0:T(1,128)}, u32[]{:S(2)}) copy-start(s32[1,48]{1,0:T(1,128)} %counts.3) | copy-start | bytes 580
  75.3 34.4 %all-to-all-start.1 = ((bf16[32,200,128]{2,1,0:T(8,128)(2,1)}), bf16[32,200,128]{2,1,0:T(8,128)(2,1)S(1)}, u32[]{:S(2)}, u32[]{:S(2)}) async-start(bf16[32,200,128]{2,1,0:T(8,128)(2,1)} %pack_v.1), calls=%async_computation.1 | async-start | bytes 3276800 | tf_op jit(solution)/shard_map/all_to_all | solution.py:339
  108.5 1.1 copy-start.3
  109.7 51.9 %all-to-all-start.3 = ((bf16[32,1,192,128]{3,2,1,0:T(8,128)(2,1)}), bf16[32,1,192,128]{3,2,1,0:T(8,128)(2,1)S(1)}, u32[]{:S(2)}, u32[]{:S(2)}) async-start(bf16[32,1,192,128]{3,2,1,0:T(8,128)(2,1)} %copy-done.3), calls=%async_computation.3 | async-start | bytes 3145728 | tf_op jit(solution)/shard_map/all_to_all | solution.py:339
  159.9 1.6 copy-start.2
  161.6 1.1 copy-start
  162.7 67.9 %all-to-all-start.2 = ((bf16[32,2,192,128]{3,2,1,0:T(8,128)(2,1)}), bf16[32,2,192,128]{3,2,1,0:T(8,128)(2,1)S(1)}, u32[]{:S(2)}, u32[]{:S(2)}) async-start(bf16[32,2,192,128]{3,2,1,0:T(8,128)(2,1)} %copy-done.2), calls=%async_computation.2 | async-start | bytes 6291456 | tf_op jit(solution)/shard_map/all_to_all | solution.py:339
  188.9 1.4 copy-start.1

commit v2 on v1

--- a/solution.py
+++ b/solution.py
@@ -16,6 +16,7 @@
 KMAX = 12
 MAXPAIR = KMAX // 2
 COLS = 4
+GROUP = 2
 SCALE = HD**-0.5
 EXP2_SCALE = SCALE * 1.4426950408889634
 NEG = -1e30
@@ -133,20 +134,62 @@
         ref[shard, part, pl.ds(start, 64), :] = value[64 * half : 64 * half + 64]
 
 
-def slot_pair(blocks, a, p, last, full):
-    i0 = blocks[a, 2 * p]
-    i1 = blocks[a, 2 * p + 1]
-    if not last:
-        return i0, i1, i1
-    return i0, jnp.where(full, i1, i0), jnp.where(full, i1, NB)
-
-
-def dead_half(full):
+def live_lanes(n, p):
     lane = lax.broadcasted_iota(jnp.int32, (1, 2 * BLK), 1)
-    return jnp.logical_and(lane >= BLK, jnp.logical_not(full))
-
-
-def first_kernel(blocks, counts, q_ref, k_ref, g_ref, dv_ref, lse_ref, acc, st, wq, wg):
+    return lane < BLK * (n - 2 * p)
+
+
+def targets(blocks, a, n, pairs):
+    return [jnp.where(s < n, blocks[a, s], NB) for s in range(2 * pairs)]
+
+
+def gather(ref, blocks, a, pairs):
+    return jnp.concatenate(
+        [
+            wide(rows(ref, blocks[a, 2 * p]), rows(ref, blocks[a, 2 * p + 1]))
+            for p in range(pairs)
+        ],
+        axis=0,
+    )
+
+
+def masked(j, p, pairs):
+    return p > 0 and (j < GROUP - 1 or p == pairs - 1)
+
+
+def add_pairs(acc, where, x, pairs):
+    for p in range(pairs):
+        piece = x[BLK * p : BLK * (p + 1)]
+        b0 = acc[where[2 * p]] + piece[:, :BLK]
+        b1 = acc[where[2 * p + 1]] + piece[:, BLK:]
+        acc[where[2 * p]] = b0
+        acc[where[2 * p + 1]] = b1
+
+
+def group_loop(order, counts, prepare, work):
+    groups = NB // GROUP
+    for j in range(GROUP):
+        prepare(0, j, order[0, j])
+
+    def body(i, carry):
+        slot = i % 2
+        ids = [order[0, GROUP * i + j] for j in range(GROUP)]
+        ns = [counts[0, a] for a in ids]
+        ahead = [order[0, GROUP * jnp.minimum(i + 1, groups - 1) + j] for j in range(GROUP)]
+
+        def run(pairs):
+            for j in range(GROUP):
+                prepare(1 - slot, j, ahead[j])
+            work(slot, ids, ns, pairs)
+
+        for pairs in range(1, MAXPAIR + 1):
+            pl.when((ns[-1] + 1) // 2 == pairs)(functools.partial(run, pairs))
+        return carry
+
+    lax.fori_loop(0, groups, body, 0)
+
+
+def first_kernel(order, blocks, counts, q_ref, k_ref, g_ref, dv_ref, lse_ref, acc, st, wq, wg):
     q = q_ref.reshape(TOKENS, HD)
     k = k_ref.reshape(TOKENS, HD)
     g = g_ref.reshape(TOKENS, HD)
@@ -154,59 +197,55 @@
     wq[...] = jnp.zeros_like(wq)
     wg[...] = jnp.zeros_like(wg)
 
-    def work(a, n, pairs):
-        full = n == 2 * pairs
-        top = None
-        ids = []
-        for p in range(pairs):
-            last = p == pairs - 1
-            i0, i1, j1 = slot_pair(blocks, a, p, last, full)
-            ids.append((i0, j1))
-            s = dot(wide(rows(k, i0), rows(k, i1)), wq[...])
-            if last:
-                s = jnp.where(dead_half(full), NEG, s)
-            st[p] = s
-            here = jnp.max(s, axis=0, keepdims=True)
-            top = here if top is None else jnp.maximum(top, here)
-        top = jnp.maximum(top[:, :BLK], top[:, BLK:]) * EXP2_SCALE
-        top2 = wide(top, top)
-        total = None
-        for p in range(pairs):
-            e = jnp.exp2(st[p] * EXP2_SCALE - top2)
-            st[p] = e
-            here = jnp.sum(e, axis=0, keepdims=True)
-            total = here if total is None else total + here
-        total = total[:, :BLK] + total[:, BLK:]
-        lse_ref[a] = top + jnp.log2(total)
-        inverse = 1.0 / total
-        inverse2 = wide(inverse, inverse)
-        for p in range(pairs):
-            dv = dot((st[p] * inverse2).astype(bf16), wg[...])
-            i0, j1 = ids[p]
-            b0 = acc[i0] + dv[:, :BLK]
-            b1 = acc[j1] + dv[:, BLK:]
-            acc[i0] = b0
-            acc[j1] = b1
-
-    def body(a, carry):
-        n = counts[0, a]
-        diagonal(wq, rows(q, a).T)
-        diagonal(wg, rows(g, a))
-        for pairs in range(1, MAXPAIR + 1):
-            pl.when((n + 1) // 2 == pairs)(functools.partial(work, a, n, pairs))
-        return carry
-
-    lax.fori_loop(0, NB, body, 0)
+    def prepare(slot, j, a):
+        diagonal(wq.at[slot, j], rows(q, a).T)
+        diagonal(wg.at[slot, j], rows(g, a))
+
+    def work(slot, ids, ns, pairs):
+        tops = []
+        for j in range(GROUP):
+            s = dot(gather(k, blocks, ids[j], pairs), wq[slot, j])
+            top = None
+            for p in range(pairs):
+                piece = s[BLK * p : BLK * (p + 1)]
+                if masked(j, p, pairs):
+                    piece = jnp.where(live_lanes(ns[j], p), piece, NEG)
+                st[j, p] = piece
+                here = jnp.max(piece, axis=0, keepdims=True)
+                top = here if top is None else jnp.maximum(top, here)
+            tops.append(jnp.maximum(top[:, :BLK], top[:, BLK:]) * EXP2_SCALE)
+        inverses = []
+        for j in range(GROUP):
+            top2 = wide(tops[j], tops[j])
+            total = None
+            for p in range(pairs):
+                e = jnp.exp2(st[j, p] * EXP2_SCALE - top2)
+                st[j, p] = e
+                here = jnp.sum(e, axis=0, keepdims=True)
+                total = here if total is None else total + here
+            total = total[:, :BLK] + total[:, BLK:]
+            lse_ref[ids[j]] = tops[j] + jnp.log2(total)
+            inverse = 1.0 / total
+            inverses.append(wide(inverse, inverse))
+        for j in range(GROUP):
+            probs = jnp.concatenate(
+                [(st[j, p] * inverses[j]).astype(bf16) for p in range(pairs)], axis=0
+            )
+            dv = dot(probs, wg[slot, j])
+            add_pairs(acc, targets(blocks, ids[j], ns[j], pairs), dv, pairs)
+
+    group_loop(order, counts, prepare, work)
 
     def finish(b, carry):
         store_block(dv_ref, 0, b, acc[b].astype(bf16))
         return carry
 
-    lax.fori_loop(0, NB, finish, 0)
+    lax.fori_loop(0, NB, finish, 0, unroll=4)
 
 
 def second_kernel(
-    blocks, counts, q_ref, k_ref, g_ref, v_ref, t_ref, lse_ref, out_ref, acc, kt, terms, wq, wg, wn
+    order, blocks, counts, q_ref, k_ref, g_ref, v_ref, t_ref, lse_ref, out_ref,
+    acc, kt, terms, ds_ref, wq, wg, wn,
 ):
     q = q_ref.reshape(TOKENS, HD)
     k = k_ref.reshape(TOKENS, HD)
@@ -217,7 +256,7 @@
     wg[...] = jnp.zeros_like(wg)
     wn[...] = jnp.zeros_like(wn)
 
-    def prepare(t, carry):
+    def row_terms(t, carry):
         a = t_ref[2 * t].astype(f32)
         b = t_ref[2 * t + 1].astype(f32)
         a0 = a[0:1] + a[2:3] + a[4:5]
@@ -231,50 +270,47 @@
             kt[3 * t + r] = rows(k, 3 * t + r).T
         return carry
 
-    lax.fori_loop(0, NB // 3, prepare, 0)
-
-    def work(a, n, pairs):
-        full = n == 2 * pairs
-        lse = wide(lse_ref[a], lse_ref[a])
-        term = wide(terms[a], terms[a])
-        dq = None
-        for p in range(pairs):
-            last = p == pairs - 1
-            i0, i1, j1 = slot_pair(blocks, a, p, last, full)
-            s = dot(wide(rows(k, i0), rows(k, i1)), wq[...])
-            dp = dot(wide(rows(v, i0), rows(v, i1)), wg[...])
-            ds = jnp.exp2(s * EXP2_SCALE - lse) * (dp - term)
-            if last:
-                ds = jnp.where(dead_half(full), 0.0, ds)
-            ds = ds.astype(bf16)
-            dk = dot(ds, wn[...])
-            b0 = acc[i0] + dk[:, :BLK]
-            b1 = acc[j1] + dk[:, BLK:]
-            acc[i0] = b0
-            acc[j1] = b1
-            part = dot(
-                wide(kt[i0], kt[i1]), jnp.concatenate([ds[:, :BLK], ds[:, BLK:]], axis=0)
+    lax.fori_loop(0, NB // 3, row_terms, 0, unroll=2)
+
+    def prepare(slot, j, a):
+        qb = rows(q, a)
+        diagonal(wq.at[slot, j], qb.T)
+        diagonal(wn.at[slot, j], qb)
+        diagonal(wg.at[slot, j], rows(g, a).T)
+
+    def work(slot, ids, ns, pairs):
+        for j in range(GROUP):
+            a = ids[j]
+            s = dot(gather(k, blocks, a, pairs), wq[slot, j])
+            dp = dot(gather(v, blocks, a, pairs), wg[slot, j])
+            lse = wide(lse_ref[a], lse_ref[a])
+            term = wide(terms[a], terms[a])
+            for p in range(pairs):
+                piece = slice(BLK * p, BLK * (p + 1))
+                probs = jnp.exp2(s[piece] * EXP2_SCALE - lse)
+                if masked(j, p, pairs):
+                    probs = jnp.where(live_lanes(ns[j], p), probs, 0.0)
+                ds = (probs * (dp[piece] - term)).astype(bf16)
+                ds_ref[j, 2 * p] = ds[:, :BLK]
+                ds_ref[j, 2 * p + 1] = ds[:, BLK:]
+        for j in range(GROUP):
+            a = ids[j]
+            ds = jnp.concatenate(
+                [wide(ds_ref[j, 2 * p], ds_ref[j, 2 * p + 1]) for p in range(pairs)], axis=0
             )
-            dq = part if dq is None else dq + part
-        store_block(out_ref, 0, a, (dq.T * SCALE).astype(bf16))
-
-    def body(a, carry):
-        n = counts[0, a]
-        qb = rows(q, a)
-        diagonal(wq, qb.T)
-        diagonal(wn, qb)
-        diagonal(wg, rows(g, a).T)
-        for pairs in range(1, MAXPAIR + 1):
-            pl.when((n + 1) // 2 == pairs)(functools.partial(work, a, n, pairs))
-        return carry
-
-    lax.fori_loop(0, NB, body, 0)
+            dk = dot(ds, wn[slot, j])
+            add_pairs(acc, targets(blocks, a, ns[j], pairs), dk, pairs)
+            keys = jnp.concatenate([kt[blocks[a, s]] for s in range(2 * pairs)], axis=1)
+            dq = dot(keys, jnp.concatenate([ds_ref[j, s] for s in range(2 * pairs)], axis=0))
+            store_block(out_ref, 0, a, (dq.T * SCALE).astype(bf16))
+
+    group_loop(order, counts, prepare, work)
 
     def finish(b, carry):
         store_block(out_ref, 1, b, (acc[b] * SCALE).astype(bf16))
         return carry
 
-    lax.fori_loop(0, NB, finish, 0)
+    lax.fori_loop(0, NB, finish, 0, unroll=4)
 
 
 def part_specs(count):
@@ -284,11 +320,11 @@
     ]
 
 
-def first_phase(blocks, counts, x):
+def first_phase(order, blocks, counts, x):
     return pl.pallas_call(
         first_kernel,
         grid=(1,),
-        in_specs=[SMEM_SPEC, SMEM_SPEC] + part_specs(3),
+        in_specs=[SMEM_SPEC] * 3 + part_specs(3),
         out_specs=[VMEM_SPEC] * 2,
         out_shape=[
             jax.ShapeDtypeStruct((SHARDS, 1, ROWS, HD), bf16),
@@ -296,23 +332,23 @@
         ],
         scratch_shapes=[
             pltpu.VMEM((NB + 1, BLK, HD), f32),
-            pltpu.VMEM((MAXPAIR, BLK, 2 * BLK), f32),
-            pltpu.VMEM((2 * BLK, 2 * BLK), bf16),
-            pltpu.VMEM((2 * BLK, 2 * BLK), bf16),
+            pltpu.VMEM((GROUP, MAXPAIR, BLK, 2 * BLK), f32),
+            pltpu.VMEM((2, GROUP, 2 * BLK, 2 * BLK), bf16),
+            pltpu.VMEM((2, GROUP, 2 * BLK, 2 * BLK), bf16),
         ],
         compiler_params=pltpu.CompilerParams(vmem_limit_bytes=40 << 20),
         cost_estimate=pl.CostEstimate(
             flops=20_000_000_000, bytes_accessed=6291456, transcendentals=5_000_000
         ),
         name="softmax_and_values",
-    )(blocks, counts, x, x, x)
-
-
-def second_phase(blocks, counts, x, v, lse):
+    )(order, blocks, counts, x, x, x)
+
+
+def second_phase(order, blocks, counts, x, v, lse):
     return pl.pallas_call(
         second_kernel,
         grid=(1,),
-        in_specs=[SMEM_SPEC, SMEM_SPEC]
+        in_specs=[SMEM_SPEC] * 3
         + part_specs(3)
         + [
             pl.BlockSpec((SHARDS, ROWS, HD), lambda _: (0, 0, 0)),
@@ -325,28 +361,38 @@
             pltpu.VMEM((NB + 1, BLK, HD), f32),
             pltpu.VMEM((NB, HD, BLK), bf16),
             pltpu.VMEM((NB, 1, BLK), f32),
+            pltpu.VMEM((GROUP, KMAX, BLK, BLK), bf16),
         ]
-        + [pltpu.VMEM((2 * BLK, 2 * BLK), bf16)] * 3,
+        + [pltpu.VMEM((2, GROUP, 2 * BLK, 2 * BLK), bf16)] * 3,
         compiler_params=pltpu.CompilerParams(vmem_limit_bytes=40 << 20),
         cost_estimate=pl.CostEstimate(
             flops=20_000_000_000, bytes_accessed=9437184, transcendentals=5_000_000
         ),
         name="scores_and_gradients",
-    )(blocks, counts, x, x, x, v, v, lse)
+    )(order, blocks, counts, x, x, x, v, v, lse)
 
 
 def exchange(x):
     return lax.all_to_all(x, "head", split_axis=0, concat_axis=0, tiled=True)
+
+
+def by_count(counts):
+    n = counts[0]
+    ids = jnp.arange(NB, dtype=jnp.int32)
+    before = (n[None, :] < n[:, None]) | ((n[None, :] == n[:, None]) & (ids[None, :] < ids[:, None]))
+    rank = jnp.sum(before.astype(jnp.int32), axis=1)
+    return jnp.sum(jnp.where(rank[None, :] == ids[:, None], ids[None, :], 0), axis=1).reshape(1, NB)
 
 
 def per_device(queries, key_vectors, values, out_grad, output, key_blocks, block_count):
     parity = (lax.axis_index("head") % 2).astype(jnp.int32).reshape(1)
     blocks = key_blocks[0]
+    order = by_count(block_count)
     x = exchange(pack(queries, key_vectors, out_grad))
     v = exchange(pack_values(parity, values, out_grad, output))
-    dv, lse = first_phase(blocks, block_count, x)
+    dv, lse = first_phase(order, blocks, block_count, x)
     (value_grad,) = unpack(exchange(dv))
-    query_grad, key_grad = unpack(exchange(second_phase(blocks, block_count, x, v, lse)))
+    query_grad, key_grad = unpack(exchange(second_phase(order, blocks, block_count, x, v, lse)))
     return query_grad, key_grad, value_grad
 
 

time: 237 us -> 195 us (0.82)
  starting transfers between devices: 50.9 us -> 29.1 us
  Pallas kernels: 87.1 us -> 67.3 us
    all_to_all x4, starting transfers between devices: 50.9 us -> 29.1 us  [exchange(): return lax.all_to_all(x, 'head', split_axis=0, concat_axis=0, tiled=True)]
    pallas_call x2, Pallas kernels: 66.4 us -> 46.6 us  [the longest x1 24.4 us: second_phase(): pl.pallas_call(second_kernel, grid=(1,), in_specs=[SMEM_SPEC] * 3 + part_...]
  transfers between devices with their start and end apart: 4 -> 4, of which waited for: 2 -> 3; matrix products, arithmetic and copies ran while one was open for 0% -> 0% of each run, Pallas kernels for 33% -> 29%
where the time goes in v2:
time: 195 us; the launch traced here: 194 us
  waiting for transfers between devices  90.9 us (47%)
  Pallas kernels  67.3 us (35%)
  starting transfers between devices  29.1 us (15%)
  local copies, waits for them, and re-layouts  5.4 us (3%)
    all_to_all x4, waiting for transfers between devices, exchange(): return lax.all_to_all(x, 'head', split_axis=0, concat_axis=0, tiled=True)  90.9 us
    all_to_all x4, starting transfers between devices, exchange(): return lax.all_to_all(x, 'head', split_axis=0, concat_axis=0, tiled=True)  29.1 us
    pallas_call x1, Pallas kernels, second_phase(): pl.pallas_call(second_kernel, grid=(1,), in_specs=[SMEM_SPEC] * 3 + part_...  24.4 us
    pallas_call x1, Pallas kernels, first_phase(): pl.pallas_call(first_kernel, grid=(1,), in_specs=[SMEM_SPEC] * 3 + part_s...  22.2 us
    pallas_call x1, Pallas kernels, pack(): pl.pallas_call(pack_kernel, grid=(SHARDS // COLS,), in_specs=[block] * 3,...  7.23 us
    pallas_call x1, Pallas kernels, pack_values(): pl.pallas_call(pack_values_kernel, grid=(SHARDS // COLS,), in_specs=[SMEM...  7.21 us
    pallas_call x2, Pallas kernels, unpack(): pl.pallas_call(unpack_kernel, grid=(SHARDS // COLS,), in_specs=[pl.BlockS...  6.26 us
    unnamed x13, local copies, waits for them, and re-layouts  5.4 us
  transfers between devices with their start and end apart: 4, of which 3 were waited for; matrix products, arithmetic and copies ran while one was open for 0% of the time, Pallas kernels for 29%

profile of v2, /device:TPU:0, one launch (start us, length us, event | category | flops | bytes accessed | tf_op | source)
XLA Modules:
  0.0 193.8 jit_solution(14299202872697570907)
XLA Ops:
  0.6 7.2 %pack_qkg.1 = bf16[32,3,192,128]{3,2,1,0:T(8,128)(2,1)} custom-call(bf16[192,4096]{1,0:T(8,128)(2,1)} %q_ref.1, bf16[192,4096]{1,0:T(8,128)(2,1)} %k_ref.1, bf16[192,4096]{1,0:T(8,128)(2,1)} %g_ref.3), custom_call_target="tpu_custom_call" | custom-call | bytes 9437184 | tf_op jit(solution)/shard_map/pack_qkg/pallas_call | solution.py:55
  7.9 0.0 copy-start.5
  7.9 7.7 %all-to-all-start = ((bf16[32,3,192,128]{3,2,1,0:T(8,128)(2,1)}), bf16[32,3,192,128]{3,2,1,0:T(8,128)(2,1)}, u32[]{:S(2)}, u32[]{:S(2)}) async-start(bf16[32,3,192,128]{3,2,1,0:T(8,128)(2,1)} %pack_qkg.1), calls=%async_computation | async-start | bytes 9437184 | tf_op jit(solution)/shard_map/all_to_all | solution.py:376
  15.5 0.0 copy-done.5
  15.5 0.1 copy.11
  15.6 0.0 copy-start.4
  15.6 7.2 %pack_v.1 = bf16[32,200,128]{2,1,0:T(8,128)(2,1)} custom-call(s32[1]{0:T(128)} %bitcast.3.parity_ref, bf16[192,4096]{1,0:T(8,128)(2,1)} %v_ref.1, bf16[192,4096]{1,0:T(8,128)(2,1)} %g_ref.3, bf16[192,4096]{1,0:T(8,128)(2,1)} %o_ref.1), custom_call_target="tpu_custom_call" | custom-call | bytes 6291456 | tf_op jit(solution)/shard_map/pack_v/pallas_call | solution.py:95
  22.8 0.0 copy-done.4
  22.8 0.2 convert_reduce_fusion
  23.0 0.1 select_reduce_fusion
  23.1 52.1 %all-to-all-done.q_ref.k_ref.g_ref = bf16[32,3,192,128]{3,2,1,0:T(8,128)(2,1)} async-done(((bf16[32,3,192,128]{3,2,1,0:T(8,128)(2,1)}), bf16[32,3,192,128]{3,2,1,0:T(8,128)(2,1)}, u32[]{:S(2)}, u32[]{:S(2)}) %all-to-all-start) | async-done | bytes 4718624 | tf_op jit(solution)/shard_map/all_to_all | solution.py:376
  75.3 4.0 %all-to-all-start.1 = ((bf16[32,200,128]{2,1,0:T(8,128)(2,1)}), bf16[32,200,128]{2,1,0:T(8,128)(2,1)S(1)}, u32[]{:S(2)}, u32[]{:S(2)}) async-start(bf16[32,200,128]{2,1,0:T(8,128)(2,1)} %pack_v.1), calls=%async_computation.1 | async-start | bytes 3276800 | tf_op jit(solution)/shard_map/all_to_all | solution.py:376
  79.2 22.2 %softmax_and_values.1 = (bf16[32,1,192,128]{3,2,1,0:T(8,128)(2,1)S(1)}, f32[48,1,128]{2,1,0:T(1,128)S(1)}) custom-call(s32[1,48]{1,0:T(1,128)S(1)} %bitcast.7, s32[48,12]{1,0:T(8,128)S(1)} %bitcast.4, s32[1,48]{1,0:T(1,128)S(1)} %copy-done.4, bf16[32,3,192,128]{3,2,1,0:T(8,128)(2,1)} %all-to-all-done.q_ref.k_ref.g_ref, ...), custom_call_target="tpu_custom_call" | custom-call | flops 20000000000 | bytes 6291456 | tf_op jit(solution)/shard_map/softmax_and_values/pallas_call | solution.py:324
  101.5 0.0 copy-start.3
  101.5 1.1 copy-done.3
  102.6 1.3 all-to-all-done.1.v_ref.t_ref
  103.9 8.0 %all-to-all-start.3 = ((bf16[32,1,192,128]{3,2,1,0:T(8,128)(2,1)}), bf16[32,1,192,128]{3,2,1,0:T(8,128)(2,1)S(1)}, u32[]{:S(2)}, u32[]{:S(2)}) async-start(bf16[32,1,192,128]{3,2,1,0:T(8,128)(2,1)} %copy-done.3), calls=%async_computation.3 | async-start | bytes 3145728 | tf_op jit(solution)/shard_map/all_to_all | solution.py:376
  111.9 24.4 %scores_and_gradients.1 = bf16[32,2,192,128]{3,2,1,0:T(8,128)(2,1)S(1)} custom-call(s32[1,48]{1,0:T(1,128)S(1)} %bitcast.8, s32[48,12]{1,0:T(8,128)S(1)} %bitcast.5, s32[1,48]{1,0:T(1,128)S(1)} %copy-done.4, bf16[32,3,192,128]{3,2,1,0:T(8,128)(2,1)} %all-to-all-done.q_ref.k_ref.g_ref, bf16[32,3,192,128]{3,2,1,0:T(8,128)(2,1)} %all-to-all-done.q_ref.k_ref.g_ref, ...), custom_call_target="tpu_custom_call" | custom-call | flops 20000000000 | bytes 9437184 | tf_op jit(solution)/shard_map/scores_and_gradients/pallas_call | solution.py:348
  136.4 0.0 copy-start.2
  136.4 1.6 copy-done.2
  138.0 0.0 all-to-all-done.3.refs_0_
  138.0 0.0 copy-start
  138.0 1.1 copy-done
  139.2 9.5 %all-to-all-start.2 = ((bf16[32,2,192,128]{3,2,1,0:T(8,128)(2,1)}), bf16[32,2,192,128]{3,2,1,0:T(8,128)(2,1)S(1)}, u32[]{:S(2)}, u32[]{:S(2)}) async-start(bf16[32,2,192,128]{3,2,1,0:T(8,128)(2,1)} %copy-done.2), calls=%async_computation.2 | async-start | bytes 6291456 | tf_op jit(solution)/shard_map/all_to_all | solution.py:376
  148.7 0.0 copy-start.1
  148.7 1.4 copy-done.1
  150.1 2.9 %unpack.3 = bf16[192,4096]{1,0:T(8,128)(2,1)} custom-call(bf16[32,1,192,128]{3,2,1,0:T(8,128)(2,1)S(1)} %copy-done.1), custom_call_target="tpu_custom_call" | custom-call | bytes 3145728 | tf_op jit(solution)/shard_map/unpack/pallas_call | solution.py:115
  153.0 37.5 %all-to-all-done.2.refs_0_ = bf16[32,2,192,128]{3,2,1,0:T(8,128)(2,1)S(1)} async-done(((bf16[32,2,192,128]{3,2,1,0:T(8,128)(2,1)}), bf16[32,2,192,128]{3,2,1,0:T(8,128)(2,1)S(1)}, u32[]{:S(2)}, u32[]{:S(2)}) %all-to-all-start.2) | async-done | bytes 3145760 | tf_op jit(solution)/shard_map/all_to_all | solution.py:376
  190.4 3.4 %unpack.2 = (bf16[192,4096]{1,0:T(8,128)(2,1)}, bf16[192,4096]{1,0:T(8,128)(2,1)}) custom-call(bf16[32,2,192,128]{3,2,1,0:T(8,128)(2,1)S(1)} %all-to-all-done.2.refs_0_), custom_call_target="tpu_custom_call" | custom-call | bytes 6291456 | tf_op jit(solution)/shard_map/unpack/pallas_call | solution.py:115
Async XLA Ops:
  7.9 7.7 %copy-start.5 = (s32[1,48,12]{1,0,2:T(1,128)S(1)}, s32[1,48,12]{1,0,2:T(1,128)}, u32[]{:S(2)}) copy-start(s32[1,48,12]{1,0,2:T(1,128)} %param.12) | copy-start | bytes 6916
  7.9 67.4 %all-to-all-start = ((bf16[32,3,192,128]{3,2,1,0:T(8,128)(2,1)}), bf16[32,3,192,128]{3,2,1,0:T(8,128)(2,1)}, u32[]{:S(2)}, u32[]{:S(2)}) async-start(bf16[32,3,192,128]{3,2,1,0:T(8,128)(2,1)} %pack_qkg.1), calls=%async_computation | async-start | bytes 9437184 | tf_op jit(solution)/shard_map/all_to_all | solution.py:376
  15.6 7.2 %copy-start.4 = (s32[1,48]{1,0:T(1,128)S(1)}, s32[1,48]{1,0:T(1,128)}, u32[]{:S(2)}) copy-start(s32[1,48]{1,0:T(1,128)} %counts.3) | copy-start | bytes 580
  75.3 28.6 %all-to-all-start.1 = ((bf16[32,200,128]{2,1,0:T(8,128)(2,1)}), bf16[32,200,128]{2,1,0:T(8,128)(2,1)S(1)}, u32[]{:S(2)}, u32[]{:S(2)}) async-start(bf16[32,200,128]{2,1,0:T(8,128)(2,1)} %pack_v.1), calls=%async_computation.1 | async-start | bytes 3276800 | tf_op jit(solution)/shard_map/all_to_all | solution.py:376
  101.5 1.1 copy-start.3
  103.9 34.1 %all-to-all-start.3 = ((bf16[32,1,192,128]{3,2,1,0:T(8,128)(2,1)}), bf16[32,1,192,128]{3,2,1,0:T(8,128)(2,1)S(1)}, u32[]{:S(2)}, u32[]{:S(2)}) async-start(bf16[32,1,192,128]{3,2,1,0:T(8,128)(2,1)} %copy-done.3), calls=%async_computation.3 | async-start | bytes 3145728 | tf_op jit(solution)/shard_map/all_to_all | solution.py:376
  136.4 1.6 copy-start.2
  138.0 1.1 copy-start
  139.2 51.3 %all-to-all-start.2 = ((bf16[32,2,192,128]{3,2,1,0:T(8,128)(2,1)}), bf16[32,2,192,128]{3,2,1,0:T(8,128)(2,1)S(1)}, u32[]{:S(2)}, u32[]{:S(2)}) async-start(bf16[32,2,192,128]{3,2,1,0:T(8,128)(2,1)} %copy-done.2), calls=%async_computation.2 | async-start | bytes 6291456 | tf_op jit(solution)/shard_map/all_to_all | solution.py:376
  148.7 1.4 copy-start.1

commit v3 on v2

v3 whole, which is shorter than its diff:
```python
import functools

import jax
import jax.numpy as jnp
from jax import lax
from jax.experimental import pallas as pl
from jax.experimental.pallas import tpu as pltpu
from jax.sharding import PartitionSpec as P

HD = 128
BLK = 128
SHARDS = 32
ROWS = 192
TERMS = 16
TOKENS = SHARDS * ROWS
NB = TOKENS // BLK
KMAX = 12
COLS = 4
WIDE = 8
STEPS = SHARDS // WIDE
OUT_STEPS = 8
GROUP = 4
STEP = 2
SCALE = HD**-0.5
EXP2_SCALE = SCALE * 1.4426950408889634
NEG = -1e30
f32 = jnp.float32
bf16 = jnp.bfloat16

VMEM_SPEC = pl.BlockSpec(memory_space=pltpu.VMEM)
ANY_SPEC = pl.BlockSpec(memory_space=pl.ANY)
HBM_SPEC = ANY_SPEC
SMEM_SPEC = pl.BlockSpec(memory_space=pltpu.SMEM)


def dot(a, b):
    return lax.dot_general(a, b, (((1,), (0,)), ((), ())), preferred_element_type=f32)


def rows(ref, i):
    return ref[pl.ds(pl.multiple_of(i * BLK, BLK), BLK), :]


def wide(a, b):
    return jnp.concatenate([a, b], axis=1)


def pack_kernel(q_ref, k_ref, g_ref, out_ref, src, dst, src_sem, dst_sem):
    parts = (q_ref, k_ref, g_ref)

    def read(c, i):
        return pltpu.make_async_copy(
            parts[i].at[:, c * WIDE * HD : (c + 1) * WIDE * HD], src.at[c, i], src_sem.at[c, i]
        )

    def write(c):
        heads = pl.ds(c * WIDE, WIDE)
        return pltpu.make_async_copy(dst.at[heads], out_ref.at[heads], dst_sem.at[c])

    for c in range(STEPS):
        for i in range(3):
            read(c, i).start()
    for c in range(STEPS):
        for i in range(3):
            read(c, i).wait()
            for j in range(WIDE):
                dst[c * WIDE + j, i] = src[c, i, :, j * HD : (j + 1) * HD]
        write(c).start()
    for c in range(STEPS):
        write(c).wait()


def pack(q, k, g):
    return pl.pallas_call(
        pack_kernel,
        in_specs=[ANY_SPEC] * 3,
        out_specs=HBM_SPEC,
        out_shape=jax.ShapeDtypeStruct((SHARDS, 3, ROWS, HD), bf16),
        scratch_shapes=[
            pltpu.VMEM((STEPS, 3, ROWS, WIDE * HD), bf16),
            pltpu.VMEM((SHARDS, 3, ROWS, HD), bf16),
            pltpu.SemaphoreType.DMA((STEPS, 3)),
            pltpu.SemaphoreType.DMA((STEPS,)),
        ],
        compiler_params=pltpu.CompilerParams(vmem_limit_bytes=60 << 20),
        cost_estimate=pl.CostEstimate(flops=0, bytes_accessed=9437184, transcendentals=0),
        name="pack_qkg",
    )(q, k, g)


def pack_values_kernel(parity_ref, v_ref, g_ref, o_ref, x_ref):
    odd = parity_ref[0] == 1
    gap = jnp.zeros((64, HD), f32)
    ones = jnp.ones((8, HD), bf16)
    sub = lax.broadcasted_iota(jnp.int32, (8, HD), 0)
    contract = (((1,), (1,)), ((), ()))
    for c in range(COLS):
        cols = slice(c * HD, (c + 1) * HD)
        x_ref[c, 0:ROWS] = v_ref[:, cols]
        prod = g_ref[:, cols].astype(f32) * o_ref[:, cols].astype(f32)
        prod = jnp.where(
            odd, jnp.concatenate([gap, prod], axis=0), jnp.concatenate([prod, gap], axis=0)
        )
        high = prod.astype(bf16)
        low = (prod - high.astype(f32)).astype(bf16)
        terms = lax.dot_general(ones, high, contract, preferred_element_type=f32)
        terms += lax.dot_general(ones, low, contract, preferred_element_type=f32)
        out = jnp.zeros((8, HD), f32)
        rest = terms
        for part in range(3):
            piece = rest.astype(bf16).astype(f32)
            rest = rest - piece
            out = jnp.where(sub == 2 * part, piece[:, :HD], out)
            out = jnp.where(sub == 2 * part + 1, piece[:, HD:], out)
        x_ref[c, ROWS : ROWS + TERMS] = jnp.concatenate([out, jnp.zeros_like(out)], axis=0).astype(bf16)


def pack_values(parity, v, g, o):
    block = pl.BlockSpec((ROWS, COLS * HD), lambda h: (0, h))
    return pl.pallas_call(
        pack_values_kernel,
        grid=(SHARDS // COLS,),
        in_specs=[SMEM_SPEC] + [block] * 3,
        out_specs=pl.BlockSpec((COLS, ROWS + TERMS, HD), lambda h: (h, 0, 0)),
        out_shape=jax.ShapeDtypeStruct((SHARDS, ROWS + TERMS, HD), bf16),
        cost_estimate=pl.CostEstimate(flops=0, bytes_accessed=6291456, transcendentals=0),
        name="pack_v",
    )(parity, v, g, o)


def unpack_kernel(count, x_ref, *refs):
    outs, (src, dst, src_sem, dst_sem) = refs[:count], refs[count:]

    def read(c):
        heads = pl.ds(c * WIDE, WIDE)
        return pltpu.make_async_copy(x_ref.at[heads], src.at[heads], src_sem.at[c])

    def write(c, i):
        return pltpu.make_async_copy(
            dst.at[c, i], outs[i].at[:, c * WIDE * HD : (c + 1) * WIDE * HD], dst_sem.at[c, i]
        )

    for c in range(STEPS):
        read(c).start()
    for c in range(STEPS):
        read(c).wait()
        for i in range(count):
            for j in range(WIDE):
                dst[c, i, :, j * HD : (j + 1) * HD] = src[c * WIDE + j, i]
            write(c, i).start()
    for c in range(STEPS):
        for i in range(count):
            write(c, i).wait()


def unpack(x):
    count = x.shape[1]
    return pl.pallas_call(
        functools.partial(unpack_kernel, count),
        in_specs=[ANY_SPEC],
        out_specs=[HBM_SPEC] * count,
        out_shape=[jax.ShapeDtypeStruct((ROWS, SHARDS * HD), bf16)] * count,
        scratch_shapes=[
            pltpu.VMEM((SHARDS, count, ROWS, HD), bf16),
            pltpu.VMEM((STEPS, count, ROWS, WIDE * HD), bf16),
            pltpu.SemaphoreType.DMA((STEPS,)),
            pltpu.SemaphoreType.DMA((STEPS, count)),
        ],
        compiler_params=pltpu.CompilerParams(vmem_limit_bytes=24 << 20),
        cost_estimate=pl.CostEstimate(
            flops=0, bytes_accessed=count * 3145728, transcendentals=0
        ),
        name="unpack",
    )(x)


def store_block(ref, part, block, value):
    for half in range(2):
        piece = 2 * block + half
        shard = piece // 3
        start = pl.multiple_of((piece - 3 * shard) * 64, 64)
        ref[shard, part, pl.ds(start, 64), :] = value[64 * half : 64 * half + 64]


def targets(blocks, a, n, slots):
    return [jnp.where(s < n, blocks[a, s], NB) for s in range(slots)]


def gather(ref, blocks, a, slots):
    return jnp.concatenate([rows(ref, blocks[a, s]) for s in range(slots)], axis=0)


def masked(j, s, slots):
    return s > 1 and (j < GROUP - 1 or s > slots - STEP)


def add_slots(acc, where, x, slots):
    for s in range(0, slots, 2):
        take = range(s, min(s + 2, slots))
        sums = [acc[where[t]] + x[BLK * t : BLK * (t + 1)] for t in take]
        for t, total in zip(take, sums):
            acc[where[t]] = total


def group_loop(order, counts, prepare, work):
    groups = NB // GROUP
    for j in range(GROUP):
        prepare(0, j, order[0, j])

    def body(i, carry):
        slot = i % 2
        ids = [order[0, GROUP * i + j] for j in range(GROUP)]
        ns = [counts[0, a] for a in ids]
        ahead = [order[0, GROUP * jnp.minimum(i + 1, groups - 1) + j] for j in range(GROUP)]

        def run(slots):
            for j in range(GROUP):
                prepare(1 - slot, j, ahead[j])
            work(slot, ids, ns, slots)

        for slots in range(2, KMAX + 1, STEP):
            pl.when((ns[-1] + STEP - 1) // STEP * STEP == slots)(functools.partial(run, slots))
        return carry

    lax.fori_loop(0, groups, body, 0)


def load(x_ref, part, buf, sem):
    copy = pltpu.make_async_copy(x_ref.at[:, part], buf, sem)
    copy.start()
    return copy


def finish(acc, scale, buf, part, out_ref, sems):
    shards = SHARDS // OUT_STEPS
    blocks = NB // OUT_STEPS
    copies = []
    for c in range(OUT_STEPS):

        def cast(b, carry):
            store_block(buf, part, b, (acc[b] * scale).astype(bf16))
            return carry

        lax.fori_loop(c * blocks, (c + 1) * blocks, cast, 0, unroll=True)
        here = pl.ds(c * shards, shards)
        copy = pltpu.make_async_copy(buf.at[here, part], out_ref.at[here, part], sems.at[c])
        copy.start()
        copies.append(copy)
    for copy in copies:
        copy.wait()


def first_kernel(
    order, blocks, counts, x_ref, dv_ref, lse_ref,
    q_buf, k_buf, g_buf, out, acc, st, wq, wg, in_sem, out_sem,
):
    copies = [load(x_ref, i, b, in_sem.at[i]) for i, b in enumerate((q_buf, k_buf, g_buf))]
    q = q_buf.reshape(TOKENS, HD)
    k = k_buf.reshape(TOKENS, HD)
    g = g_buf.reshape(TOKENS, HD)
    acc[...] = jnp.zeros_like(acc)
    for copy in copies:
        copy.wait()

    def prepare(slot, j, a):
        wq[slot, j] = rows(q, a).T
        wg[slot, j] = rows(g, a)

    def work(slot, ids, ns, slots):
        tops = []
        for j in range(GROUP):
            scores = dot(gather(k, blocks, ids[j], slots), wq[slot, j])
            top = None
            for s in range(slots):
                piece = scores[BLK * s : BLK * (s + 1)]
                if masked(j, s, slots):
                    piece = jnp.where(s < ns[j], piece, NEG)
                st[j, s] = piece
                here = jnp.max(piece, axis=0, keepdims=True)
                top = here if top is None else jnp.maximum(top, here)
            tops.append(top * EXP2_SCALE)
        inverses = []
        for j in range(GROUP):
            total = None
            for s in range(slots):
                e = jnp.exp2(st[j, s] * EXP2_SCALE - tops[j])
                st[j, s] = e
                here = jnp.sum(e, axis=0, keepdims=True)
                total = here if total is None else total + here
            lse_ref[ids[j]] = tops[j] + jnp.log2(total)
            inverses.append(1.0 / total)
        for j in range(GROUP):
            probs = jnp.concatenate(
                [(st[j, s] * inverses[j]).astype(bf16) for s in range(slots)], axis=0
            )
            dv = dot(probs, wg[slot, j])
            add_slots(acc, targets(blocks, ids[j], ns[j], slots), dv, slots)

    group_loop(order, counts, prepare, work)

    finish(acc, 1.0, out, 0, dv_ref, out_sem)


def second_kernel(
    order, blocks, counts, x_ref, v_ref, lse_ref, out_ref,
    q_buf, k_buf, g_buf, v_buf, t_ref, out, acc, kt, terms, ds_ref, wq, wg, wn, in_sem, out_sem,
):
    k_copy = load(x_ref, 1, k_buf, in_sem.at[0])
    t_copy = load(v_ref, pl.ds(ROWS, TERMS), t_ref, in_sem.at[1])
    copies = [
        load(x_ref, 0, q_buf, in_sem.at[2]),
        load(x_ref, 2, g_buf, in_sem.at[3]),
        load(v_ref, pl.ds(0, ROWS), v_buf, in_sem.at[4]),
    ]
    q = q_buf.reshape(TOKENS, HD)
    k = k_buf.reshape(TOKENS, HD)
    g = g_buf.reshape(TOKENS, HD)
    v = v_buf.reshape(TOKENS, HD)
    acc[...] = jnp.zeros_like(acc)
    k_copy.wait()
    t_copy.wait()

    def row_terms(t, carry):
        a = t_ref[2 * t].astype(f32)
        b = t_ref[2 * t + 1].astype(f32)
        a0 = a[0:1] + a[2:3] + a[4:5]
        a1 = a[1:2] + a[3:4] + a[5:6]
        b0 = b[0:1] + b[2:3] + b[4:5]
        b1 = b[1:2] + b[3:4] + b[5:6]
        terms[3 * t] = a0
        terms[3 * t + 1] = a1 + b0
        terms[3 * t + 2] = b1
        for r in range(3):
            kt[3 * t + r] = rows(k, 3 * t + r).T
        return carry

    lax.fori_loop(0, NB // 3, row_terms, 0, unroll=4)
    for copy in copies:
        copy.wait()

    def prepare(slot, j, a):
        qb = rows(q, a)
        wq[slot, j] = qb.T
        wn[slot, j] = qb
        wg[slot, j] = rows(g, a).T

    def work(slot, ids, ns, slots):
        for j in range(GROUP):
            a = ids[j]
            scores = dot(gather(k, blocks, a, slots), wq[slot, j])
            dp = dot(gather(v, blocks, a, slots), wg[slot, j])
            lse = lse_ref[a]
            term = terms[a]
            for s in range(slots):
                piece = slice(BLK * s, BLK * (s + 1))
                probs = jnp.exp2(scores[piece] * EXP2_SCALE - lse)
                if masked(j, s, slots):
                    probs = jnp.where(s < ns[j], probs, 0.0)
                ds_ref[j, s] = (probs * (dp[piece] - term)).astype(bf16)
        for j in range(GROUP):
            a = ids[j]
            ds = jnp.concatenate([ds_ref[j, s] for s in range(slots)], axis=0)
            dk = dot(ds, wn[slot, j])
            add_slots(acc, targets(blocks, a, ns[j], slots), dk, slots)
            keys = jnp.concatenate([kt[blocks[a, s]] for s in range(slots)], axis=1)
            dq = dot(keys, jnp.concatenate([ds_ref[j, s] for s in range(slots)], axis=0))
            store_block(out, 0, a, (dq.T * SCALE).astype(bf16))

    group_loop(order, counts, prepare, work)

    dq_copy = pltpu.make_async_copy(out.at[:, 0], out_ref.at[:, 0], out_sem.at[OUT_STEPS])
    dq_copy.start()
    finish(acc, SCALE, out, 1, out_ref, out_sem)
    dq_copy.wait()


def first_phase(order, blocks, counts, x):
    return pl.pallas_call(
        first_kernel,
        in_specs=[SMEM_SPEC] * 3 + [ANY_SPEC],
        out_specs=[HBM_SPEC, VMEM_SPEC],
        out_shape=[
            jax.ShapeDtypeStruct((SHARDS, 1, ROWS, HD), bf16),
            jax.ShapeDtypeStruct((NB, 1, BLK), f32),
        ],
        scratch_shapes=[pltpu.VMEM((SHARDS, ROWS, HD), bf16)] * 3
        + [
            pltpu.VMEM((SHARDS, 1, ROWS, HD), bf16),
            pltpu.VMEM((NB + 1, BLK, HD), f32),
            pltpu.VMEM((GROUP, KMAX, BLK, BLK), f32),
            pltpu.VMEM((2, GROUP, BLK, BLK), bf16),
            pltpu.VMEM((2, GROUP, BLK, BLK), bf16),
            pltpu.SemaphoreType.DMA((3,)),
            pltpu.SemaphoreType.DMA((OUT_STEPS,)),
        ],
        compiler_params=pltpu.CompilerParams(vmem_limit_bytes=60 << 20),
        cost_estimate=pl.CostEstimate(
            flops=20_000_000_000, bytes_accessed=6291456, transcendentals=5_000_000
        ),
        name="softmax_and_values",
    )(order, blocks, counts, x)


def second_phase(order, blocks, counts, x, v, lse):
    return pl.pallas_call(
        second_kernel,
        in_specs=[SMEM_SPEC] * 3 + [ANY_SPEC] * 2 + [VMEM_SPEC],
        out_specs=HBM_SPEC,
        out_shape=jax.ShapeDtypeStruct((SHARDS, 2, ROWS, HD), bf16),
        scratch_shapes=[pltpu.VMEM((SHARDS, ROWS, HD), bf16)] * 4
        + [
            pltpu.VMEM((SHARDS, TERMS, HD), bf16),
            pltpu.VMEM((SHARDS, 2, ROWS, HD), bf16),
            pltpu.VMEM((NB + 1, BLK, HD), f32),
            pltpu.VMEM((NB, HD, BLK), bf16),
            pltpu.VMEM((NB, 1, BLK), f32),
            pltpu.VMEM((GROUP, KMAX, BLK, BLK), bf16),
        ]
        + [pltpu.VMEM((2, GROUP, BLK, BLK), bf16)] * 3
        + [pltpu.SemaphoreType.DMA((5,)), pltpu.SemaphoreType.DMA((OUT_STEPS + 1,))],
        compiler_params=pltpu.CompilerParams(vmem_limit_bytes=48 << 20),
        cost_estimate=pl.CostEstimate(
            flops=20_000_000_000, bytes_accessed=9437184, transcendentals=5_000_000
        ),
        name="scores_and_gradients",
    )(order, blocks, counts, x, v, lse)


def exchange(x):
    return lax.all_to_all(x, "head", split_axis=0, concat_axis=0, tiled=True)


def by_count(counts):
    n = counts[0]
    ids = jnp.arange(NB, dtype=jnp.int32)
    before = (n[None, :] < n[:, None]) | ((n[None, :] == n[:, None]) & (ids[None, :] < ids[:, None]))
    rank = jnp.sum(before.astype(jnp.int32), axis=1)
    return jnp.sum(jnp.where(rank[None, :] == ids[:, None], ids[None, :], 0), axis=1).reshape(1, NB)


def per_device(queries, key_vectors, values, out_grad, output, key_blocks, block_count):
    parity = (lax.axis_index("head") % 2).astype(jnp.int32).reshape(1)
    blocks = key_blocks[0]
    order = by_count(block_count)
    x = exchange(pack(queries, key_vectors, out_grad))
    v = exchange(pack_values(parity, values, out_grad, output))
    dv, lse = first_phase(order, blocks, block_count, x)
    (value_grad,) = unpack(exchange(dv))
    query_grad, key_grad = unpack(exchange(second_phase(order, blocks, block_count, x, v, lse)))
    return query_grad, key_grad, value_grad


def solution(mesh):
    token = P(("dp", "head"), None)
    return jax.shard_map(
        per_device,
        mesh=mesh,
        in_specs=(token,) * 5 + (P(("dp", "head"), None, None), token),
        out_specs=(token,) * 3,
        check_vma=False,
    )
```

time: 195 us -> 182 us (0.933)
  Pallas kernels: 67.3 us -> 52.7 us
  waiting for transfers between devices: 90.9 us -> 99.3 us
  starting transfers between devices: 29.1 us -> 21.3 us
    pallas_call x5, Pallas kernels: 60.1 us -> 45.5 us  [the longest x1 19 us: second_phase(): pl.pallas_call(second_kernel, in_specs=[SMEM_SPEC] * 3 + [ANY_SPEC] * 2 +...]
    all_to_all x4, waiting for transfers between devices: 90.9 us -> 99.3 us  [exchange(): return lax.all_to_all(x, 'head', split_axis=0, concat_axis=0, tiled=True)]
    all_to_all x4, starting transfers between devices: 29.1 us -> 21.3 us  [exchange(): return lax.all_to_all(x, 'head', split_axis=0, concat_axis=0, tiled=True)]
    unnamed x13 -> x19, local copies, waits for them, and re-layouts: 5.4 us -> 4.89 us
  transfers between devices with their start and end apart: 4 -> 4, of which waited for: 3 -> 4; matrix products, arithmetic and copies ran while one was open for 0% -> 1% of each run, Pallas kernels for 29% -> 26%
where the time goes in v3:
time: 182 us; the launch traced here: 180 us
  waiting for transfers between devices  99.3 us (55%)
  Pallas kernels  52.7 us (29%)
  starting transfers between devices  21.3 us (12%)
  local copies, waits for them, and re-layouts  4.89 us (3%)
    all_to_all x4, waiting for transfers between devices, exchange(): return lax.all_to_all(x, 'head', split_axis=0, concat_axis=0, tiled=True)  99.3 us
    all_to_all x4, starting transfers between devices, exchange(): return lax.all_to_all(x, 'head', split_axis=0, concat_axis=0, tiled=True)  21.3 us
    pallas_call x1, Pallas kernels, second_phase(): pl.pallas_call(second_kernel, in_specs=[SMEM_SPEC] * 3 + [ANY_SPEC] * 2 +...  19 us
    pallas_call x1, Pallas kernels, first_phase(): pl.pallas_call(first_kernel, in_specs=[SMEM_SPEC] * 3 + [ANY_SPEC], out_s...  18.4 us
    pallas_call x1, Pallas kernels, pack_values(): pl.pallas_call(pack_values_kernel, grid=(SHARDS // COLS,), in_specs=[SMEM...  7.21 us
    unnamed x19, local copies, waits for them, and re-layouts  4.89 us
    pallas_call x2, Pallas kernels, unpack(): pl.pallas_call(functools.partial(unpack_kernel, count), in_specs=[ANY_SPE...  4.13 us
    pallas_call x1, Pallas kernels, pack(): pl.pallas_call(pack_kernel, in_specs=[ANY_SPEC] * 3, out_specs=HBM_SPEC,...  3.92 us
  transfers between devices with their start and end apart: 4, of which 4 were waited for; matrix products, arithmetic and copies ran while one was open for 1% of the time, Pallas kernels for 26%

profile of v3, /device:TPU:0, one launch (start us, length us, event | category | flops | bytes accessed | tf_op | source)
XLA Modules:
  0.0 180.0 jit_solution(9996554141369267418)
XLA Ops:
  0.6 3.9 %pack_qkg.1 = bf16[32,3,192,128]{3,2,1,0:T(8,128)(2,1)} custom-call(bf16[192,4096]{1,0:T(8,128)(2,1)} %q_ref.1, bf16[192,4096]{1,0:T(8,128)(2,1)} %k_ref.1, bf16[192,4096]{1,0:T(8,128)(2,1)} %g_ref.3), custom_call_target="tpu_custom_call" | custom-call | bytes 9437184 | tf_op jit(solution)/shard_map/pack_qkg/pallas_call | solution.py:74
  4.6 0.0 copy-start.8
  4.6 7.5 %all-to-all-start = ((bf16[32,3,192,128]{3,2,1,0:T(8,128)(2,1)}), bf16[32,3,192,128]{3,2,1,0:T(8,128)(2,1)}, u32[]{:S(2)}, u32[]{:S(2)}) async-start(bf16[32,3,192,128]{3,2,1,0:T(8,128)(2,1)} %pack_qkg.1), calls=%async_computation | async-start | bytes 9437184 | tf_op jit(solution)/shard_map/all_to_all | solution.py:430
  12.1 0.0 copy-done.8
  12.1 0.7 copy.11
  12.8 0.0 copy-start.4
  12.8 7.2 %pack_v.1 = bf16[32,208,128]{2,1,0:T(8,128)(2,1)} custom-call(s32[1]{0:T(128)} %bitcast.3.parity_ref, bf16[192,4096]{1,0:T(8,128)(2,1)} %v_ref.1, bf16[192,4096]{1,0:T(8,128)(2,1)} %g_ref.3, bf16[192,4096]{1,0:T(8,128)(2,1)} %o_ref.1), custom_call_target="tpu_custom_call" | custom-call | bytes 6291456 | tf_op jit(solution)/shard_map/pack_v/pallas_call | solution.py:120
  20.0 0.0 copy-done.4
  20.0 0.2 convert_reduce_fusion
  20.2 0.7 select_reduce_fusion
  20.9 51.0 %all-to-all-done.x_ref = bf16[32,3,192,128]{3,2,1,0:T(8,128)(2,1)} async-done(((bf16[32,3,192,128]{3,2,1,0:T(8,128)(2,1)}), bf16[32,3,192,128]{3,2,1,0:T(8,128)(2,1)}, u32[]{:S(2)}, u32[]{:S(2)}) %all-to-all-start) | async-done | bytes 4718624 | tf_op jit(solution)/shard_map/all_to_all | solution.py:430
  71.8 4.0 %all-to-all-start.1 = ((bf16[32,208,128]{2,1,0:T(8,128)(2,1)}), bf16[32,208,128]{2,1,0:T(8,128)(2,1)S(1)}, u32[]{:S(2)}, u32[]{:S(2)}) async-start(bf16[32,208,128]{2,1,0:T(8,128)(2,1)} %pack_v.1), calls=%async_computation.1 | async-start | bytes 3407872 | tf_op jit(solution)/shard_map/all_to_all | solution.py:430
  75.8 18.4 %softmax_and_values.1 = (bf16[32,1,192,128]{3,2,1,0:T(8,128)(2,1)}, f32[48,1,128]{2,1,0:T(1,128)}) custom-call(s32[1,48]{1,0:T(1,128)} %bitcast.7, s32[48,12]{1,0:T(8,128)} %bitcast.4, s32[1,48]{1,0:T(1,128)} %counts.3, bf16[32,3,192,128]{3,2,1,0:T(8,128)(2,1)} %all-to-all-done.x_ref), custom_call_target="tpu_custom_call" | custom-call | flops 20000000000 | bytes 6291456 | tf_op jit(solution)/shard_map/softmax_and_values/pallas_call | solution.py:378
  94.3 6.9 %all-to-all-done.1.v_ref = bf16[32,208,128]{2,1,0:T(8,128)(2,1)S(1)} async-done(((bf16[32,208,128]{2,1,0:T(8,128)(2,1)}), bf16[32,208,128]{2,1,0:T(8,128)(2,1)S(1)}, u32[]{:S(2)}, u32[]{:S(2)}) %all-to-all-start.1) | async-done | bytes 1703968 | tf_op jit(solution)/shard_map/all_to_all | solution.py:430
  101.2 0.0 copy-start.3
  101.2 0.0 copy-start.5
  101.2 0.0 copy-start.6
  101.2 0.0 copy-start.7
  101.2 4.3 %all-to-all-start.3 = ((bf16[32,1,192,128]{3,2,1,0:T(8,128)(2,1)}), bf16[32,1,192,128]{3,2,1,0:T(8,128)(2,1)S(1)}, u32[]{:S(2)}, u32[]{:S(2)}) async-start(bf16[32,1,192,128]{3,2,1,0:T(8,128)(2,1)} %get-tuple-element.10), calls=%async_computation.3 | async-start | bytes 3145728 | tf_op jit(solution)/shard_map/all_to_all | solution.py:430
  105.5 0.0 copy-done.3
  105.6 0.0 copy-done.5
  105.6 0.0 copy-done.6
  105.6 0.0 copy-done.7
  105.6 19.0 %scores_and_gradients.1 = bf16[32,2,192,128]{3,2,1,0:T(8,128)(2,1)S(1)} custom-call(s32[1,48]{1,0:T(1,128)S(1)} %bitcast.8, s32[48,12]{1,0:T(8,128)S(1)} %bitcast.5, s32[1,48]{1,0:T(1,128)S(1)} %copy-done.5, bf16[32,3,192,128]{3,2,1,0:T(8,128)(2,1)} %all-to-all-done.x_ref, bf16[32,208,128]{2,1,0:T(8,128)(2,1)S(1)} %all-to-all-done.1.v_ref, ...), custom_call_target="tpu_custom_call" | custom-call | flops 20000000000 | bytes 9437184 | tf_op jit(solution)/shard_map/scores_and_gradients/pallas_call | solution.py:405
  124.6 0.0 copy-start.2
  124.6 1.6 copy-done.2
  126.2 3.1 %all-to-all-done.3.x_ref = bf16[32,1,192,128]{3,2,1,0:T(8,128)(2,1)S(1)} async-done(((bf16[32,1,192,128]{3,2,1,0:T(8,128)(2,1)}), bf16[32,1,192,128]{3,2,1,0:T(8,128)(2,1)S(1)}, u32[]{:S(2)}, u32[]{:S(2)}) %all-to-all-start.3) | async-done | bytes 1572896 | tf_op jit(solution)/shard_map/all_to_all | solution.py:430
  129.3 0.0 copy-start
  129.3 1.1 copy-done
  130.4 5.5 %all-to-all-start.2 = ((bf16[32,2,192,128]{3,2,1,0:T(8,128)(2,1)}), bf16[32,2,192,128]{3,2,1,0:T(8,128)(2,1)S(1)}, u32[]{:S(2)}, u32[]{:S(2)}) async-start(bf16[32,2,192,128]{3,2,1,0:T(8,128)(2,1)} %copy-done.2), calls=%async_computation.2 | async-start | bytes 6291456 | tf_op jit(solution)/shard_map/all_to_all | solution.py:430
  135.9 0.0 copy-start.1
  136.0 1.4 copy-done.1
  137.4 2.1 %unpack.3 = bf16[192,4096]{1,0:T(8,128)(2,1)} custom-call(bf16[32,1,192,128]{3,2,1,0:T(8,128)(2,1)S(1)} %copy-done.1), custom_call_target="tpu_custom_call" | custom-call | bytes 3145728 | tf_op jit(solution)/shard_map/unpack/pallas_call | solution.py:158
  139.4 38.3 %all-to-all-done.2.x_ref = bf16[32,2,192,128]{3,2,1,0:T(8,128)(2,1)S(1)} async-done(((bf16[32,2,192,128]{3,2,1,0:T(8,128)(2,1)}), bf16[32,2,192,128]{3,2,1,0:T(8,128)(2,1)S(1)}, u32[]{:S(2)}, u32[]{:S(2)}) %all-to-all-start.2) | async-done | bytes 3145760 | tf_op jit(solution)/shard_map/all_to_all | solution.py:430
  177.7 2.1 %unpack.2 = (bf16[192,4096]{1,0:T(8,128)(2,1)}, bf16[192,4096]{1,0:T(8,128)(2,1)}) custom-call(bf16[32,2,192,128]{3,2,1,0:T(8,128)(2,1)S(1)} %all-to-all-done.2.x_ref), custom_call_target="tpu_custom_call" | custom-call | bytes 6291456 | tf_op jit(solution)/shard_map/unpack/pallas_call | solution.py:158
Async XLA Ops:
  4.6 7.6 %copy-start.8 = (s32[1,48,12]{1,0,2:T(1,128)S(1)}, s32[1,48,12]{1,0,2:T(1,128)}, u32[]{:S(2)}) copy-start(s32[1,48,12]{1,0,2:T(1,128)} %param.12) | copy-start | bytes 6916
  4.6 67.3 %all-to-all-start = ((bf16[32,3,192,128]{3,2,1,0:T(8,128)(2,1)}), bf16[32,3,192,128]{3,2,1,0:T(8,128)(2,1)}, u32[]{:S(2)}, u32[]{:S(2)}) async-start(bf16[32,3,192,128]{3,2,1,0:T(8,128)(2,1)} %pack_qkg.1), calls=%async_computation | async-start | bytes 9437184 | tf_op jit(solution)/shard_map/all_to_all | solution.py:430
  12.8 7.2 %copy-start.4 = (s32[1,48]{1,0:T(1,128)S(1)}, s32[1,48]{1,0:T(1,128)}, u32[]{:S(2)}) copy-start(s32[1,48]{1,0:T(1,128)} %counts.3) | copy-start | bytes 580
  71.8 29.4 %all-to-all-start.1 = ((bf16[32,208,128]{2,1,0:T(8,128)(2,1)}), bf16[32,208,128]{2,1,0:T(8,128)(2,1)S(1)}, u32[]{:S(2)}, u32[]{:S(2)}) async-start(bf16[32,208,128]{2,1,0:T(8,128)(2,1)} %pack_v.1), calls=%async_computation.1 | async-start | bytes 3407872 | tf_op jit(solution)/shard_map/all_to_all | solution.py:430
  101.2 4.3 %copy-start.3 = (s32[1,48,12]{2,1,0:T(8,128)S(1)}, s32[1,48,12]{2,1,0:T(8,128)}, u32[]{:S(2)}) copy-start(s32[1,48,12]{2,1,0:T(8,128)} %copy.11) | copy-start | bytes 6916
  101.2 4.3 %copy-start.5 = (s32[1,48]{1,0:T(1,128)S(1)}, s32[1,48]{1,0:T(1,128)}, u32[]{:S(2)}) copy-start(s32[1,48]{1,0:T(1,128)} %counts.3) | copy-start | bytes 580
  101.2 4.3 %copy-start.6 = (s32[48]{0:T(128)S(1)}, s32[48]{0:T(128)}, u32[]{:S(2)}) copy-start(s32[48]{0:T(128)} %select_reduce_fusion) | copy-start | bytes 580
  101.2 4.3 %copy-start.7 = (f32[48,1,128]{2,1,0:T(1,128)S(1)}, f32[48,1,128]{2,1,0:T(1,128)}, u32[]{:S(2)}) copy-start(f32[48,1,128]{2,1,0:T(1,128)} %get-tuple-element.7.lse_ref) | copy-start | bytes 73732
  101.2 28.1 %all-to-all-start.3 = ((bf16[32,1,192,128]{3,2,1,0:T(8,128)(2,1)}), bf16[32,1,192,128]{3,2,1,0:T(8,128)(2,1)S(1)}, u32[]{:S(2)}, u32[]{:S(2)}) async-start(bf16[32,1,192,128]{3,2,1,0:T(8,128)(2,1)} %get-tuple-element.10), calls=%async_computation.3 | async-start | bytes 3145728 | tf_op jit(solution)/shard_map/all_to_all | solution.py:430
  124.6 1.6 copy-start.2
  129.3 1.1 copy-start
  130.4 47.3 %all-to-all-start.2 = ((bf16[32,2,192,128]{3,2,1,0:T(8,128)(2,1)}), bf16[32,2,192,128]{3,2,1,0:T(8,128)(2,1)S(1)}, u32[]{:S(2)}, u32[]{:S(2)}) async-start(bf16[32,2,192,128]{3,2,1,0:T(8,128)(2,1)} %copy-done.2), calls=%async_computation.2 | async-start | bytes 6291456 | tf_op jit(solution)/shard_map/all_to_all | solution.py:430
  135.9 1.4 copy-start.1

commit v4 on v3

--- a/solution.py
+++ b/solution.py
@@ -19,7 +19,7 @@
 WIDE = 8
 STEPS = SHARDS // WIDE
 OUT_STEPS = 8
-GROUP = 4
+GROUP = 6
 STEP = 2
 SCALE = HD**-0.5
 EXP2_SCALE = SCALE * 1.4426950408889634
@@ -75,7 +75,7 @@
         pack_kernel,
         in_specs=[ANY_SPEC] * 3,
         out_specs=HBM_SPEC,
-        out_shape=jax.ShapeDtypeStruct((SHARDS, 3, ROWS, HD), bf16),
+        out_shape=pltpu.HBM((SHARDS, 3, ROWS, HD), bf16),
         scratch_shapes=[
             pltpu.VMEM((STEPS, 3, ROWS, WIDE * HD), bf16),
             pltpu.VMEM((SHARDS, 3, ROWS, HD), bf16),
@@ -250,9 +250,16 @@
         copy.wait()
 
 
+def in_turn(*stages):
+    for t in range(GROUP + len(stages) - 1):
+        for d, stage in enumerate(stages):
+            if 0 <= t - d < GROUP:
+                stage(t - d)
+
+
 def first_kernel(
     order, blocks, counts, x_ref, dv_ref, lse_ref,
-    q_buf, k_buf, g_buf, out, acc, st, wq, wg, in_sem, out_sem,
+    q_buf, k_buf, g_buf, out, acc, st, wq, in_sem, out_sem,
 ):
     copies = [load(x_ref, i, b, in_sem.at[i]) for i, b in enumerate((q_buf, k_buf, g_buf))]
     q = q_buf.reshape(TOKENS, HD)
@@ -264,11 +271,11 @@
 
     def prepare(slot, j, a):
         wq[slot, j] = rows(q, a).T
-        wg[slot, j] = rows(g, a)
 
     def work(slot, ids, ns, slots):
-        tops = []
-        for j in range(GROUP):
+        tops, inverses = {}, {}
+
+        def score(j):
             scores = dot(gather(k, blocks, ids[j], slots), wq[slot, j])
             top = None
             for s in range(slots):
@@ -278,9 +285,9 @@
                 st[j, s] = piece
                 here = jnp.max(piece, axis=0, keepdims=True)
                 top = here if top is None else jnp.maximum(top, here)
-            tops.append(top * EXP2_SCALE)
-        inverses = []
-        for j in range(GROUP):
+            tops[j] = top * EXP2_SCALE
+
+        def weigh(j):
             total = None
             for s in range(slots):
                 e = jnp.exp2(st[j, s] * EXP2_SCALE - tops[j])
@@ -288,13 +295,16 @@
                 here = jnp.sum(e, axis=0, keepdims=True)
                 total = here if total is None else total + here
             lse_ref[ids[j]] = tops[j] + jnp.log2(total)
-            inverses.append(1.0 / total)
-        for j in range(GROUP):
+            inverses[j] = 1.0 / total
+
+        def add(j):
             probs = jnp.concatenate(
                 [(st[j, s] * inverses[j]).astype(bf16) for s in range(slots)], axis=0
             )
-            dv = dot(probs, wg[slot, j])
+            dv = dot(probs, rows(g, ids[j]))
             add_slots(acc, targets(blocks, ids[j], ns[j], slots), dv, slots)
+
+        in_turn(score, weigh, add)
 
     group_loop(order, counts, prepare, work)
 
@@ -380,7 +390,7 @@
         in_specs=[SMEM_SPEC] * 3 + [ANY_SPEC],
         out_specs=[HBM_SPEC, VMEM_SPEC],
         out_shape=[
-            jax.ShapeDtypeStruct((SHARDS, 1, ROWS, HD), bf16),
+            pltpu.HBM((SHARDS, 1, ROWS, HD), bf16),
             jax.ShapeDtypeStruct((NB, 1, BLK), f32),
         ],
         scratch_shapes=[pltpu.VMEM((SHARDS, ROWS, HD), bf16)] * 3
@@ -389,11 +399,10 @@
             pltpu.VMEM((NB + 1, BLK, HD), f32),
             pltpu.VMEM((GROUP, KMAX, BLK, BLK), f32),
             pltpu.VMEM((2, GROUP, BLK, BLK), bf16),
-            pltpu.VMEM((2, GROUP, BLK, BLK), bf16),
             pltpu.SemaphoreType.DMA((3,)),
             pltpu.SemaphoreType.DMA((OUT_STEPS,)),
         ],
-        compiler_params=pltpu.CompilerParams(vmem_limit_bytes=60 << 20),
+        compiler_params=pltpu.CompilerParams(vmem_limit_bytes=40 << 20),
         cost_estimate=pl.CostEstimate(
             flops=20_000_000_000, bytes_accessed=6291456, transcendentals=5_000_000
         ),
@@ -406,7 +415,7 @@
         second_kernel,
         in_specs=[SMEM_SPEC] * 3 + [ANY_SPEC] * 2 + [VMEM_SPEC],
         out_specs=HBM_SPEC,
-        out_shape=jax.ShapeDtypeStruct((SHARDS, 2, ROWS, HD), bf16),
+        out_shape=pltpu.HBM((SHARDS, 2, ROWS, HD), bf16),
         scratch_shapes=[pltpu.VMEM((SHARDS, ROWS, HD), bf16)] * 4
         + [
             pltpu.VMEM((SHARDS, TERMS, HD), bf16),
@@ -418,7 +427,7 @@
         ]
         + [pltpu.VMEM((2, GROUP, BLK, BLK), bf16)] * 3
         + [pltpu.SemaphoreType.DMA((5,)), pltpu.SemaphoreType.DMA((OUT_STEPS + 1,))],
-        compiler_params=pltpu.CompilerParams(vmem_limit_bytes=48 << 20),
+        compiler_params=pltpu.CompilerParams(vmem_limit_bytes=40 << 20),
         cost_estimate=pl.CostEstimate(
             flops=20_000_000_000, bytes_accessed=9437184, transcendentals=5_000_000
         ),

time: 182 us -> 181 us (level)
  waiting for transfers between devices: 99.3 us -> 108 us
  Pallas kernels: 52.7 us -> 47 us
  local copies, waits for them, and re-layouts: 4.89 us -> 2.65 us
    all_to_all x4, waiting for transfers between devices: 99.3 us -> 108 us  [exchange(): return lax.all_to_all(x, 'head', split_axis=0, concat_axis=0, tiled=True)]
    pallas_call x1, Pallas kernels: 18.4 us -> 14.8 us  [first_phase(): pl.pallas_call(first_kernel, in_specs=[SMEM_SPEC] * 3 + [ANY_SPEC], out_s...]
    unnamed x19 -> x9, local copies, waits for them, and re-layouts: 4.89 us -> 2.65 us
    pallas_call x1, Pallas kernels: 19 us -> 16.9 us  [second_phase(): pl.pallas_call(second_kernel, in_specs=[SMEM_SPEC] * 3 + [ANY_SPEC] * 2 +...]
  transfers between devices with their start and end apart: 4 -> 4, of which waited for: 4 -> 4; matrix products, arithmetic and copies ran while one was open for 1% -> 0% of each run, Pallas kernels for 26% -> 23%
where the time goes in v4:
time: 181 us; the launch traced here: 179 us
  waiting for transfers between devices  108 us (60%)
  Pallas kernels  47 us (26%)
  starting transfers between devices  20.3 us (11%)
  local copies, waits for them, and re-layouts  2.65 us (1%)
    all_to_all x4, waiting for transfers between devices, exchange(): return lax.all_to_all(x, 'head', split_axis=0, concat_axis=0, tiled=True)  108 us
    all_to_all x4, starting transfers between devices, exchange(): return lax.all_to_all(x, 'head', split_axis=0, concat_axis=0, tiled=True)  20.3 us
    pallas_call x1, Pallas kernels, second_phase(): pl.pallas_call(second_kernel, in_specs=[SMEM_SPEC] * 3 + [ANY_SPEC] * 2 +...  16.9 us
    pallas_call x1, Pallas kernels, first_phase(): pl.pallas_call(first_kernel, in_specs=[SMEM_SPEC] * 3 + [ANY_SPEC], out_s...  14.8 us
    pallas_call x1, Pallas kernels, pack_values(): pl.pallas_call(pack_values_kernel, grid=(SHARDS // COLS,), in_specs=[SMEM...  7.22 us
    pallas_call x2, Pallas kernels, unpack(): pl.pallas_call(functools.partial(unpack_kernel, count), in_specs=[ANY_SPE...  4.13 us
    pallas_call x1, Pallas kernels, pack(): pl.pallas_call(pack_kernel, in_specs=[ANY_SPEC] * 3, out_specs=HBM_SPEC,...  3.93 us
  transfers between devices with their start and end apart: 4, of which 4 were waited for; matrix products, arithmetic and copies ran while one was open for 0% of the time, Pallas kernels for 23%

profile of v4, /device:TPU:0, one launch (start us, length us, event | category | flops | bytes accessed | tf_op | source)
XLA Modules:
  0.0 179.0 jit_solution(10574994334691731861)
XLA Ops:
  0.6 3.9 %pack_qkg.1 = bf16[32,3,192,128]{3,2,1,0:T(8,128)(2,1)} custom-call(bf16[192,4096]{1,0:T(8,128)(2,1)} %q_ref.1, bf16[192,4096]{1,0:T(8,128)(2,1)} %k_ref.1, bf16[192,4096]{1,0:T(8,128)(2,1)} %g_ref.3), custom_call_target="tpu_custom_call" | custom-call | bytes 9437184 | tf_op jit(solution)/shard_map/pack_qkg/pallas_call | solution.py:74
  4.6 0.0 copy-start.3
  4.6 7.5 %all-to-all-start = ((bf16[32,3,192,128]{3,2,1,0:T(8,128)(2,1)}), bf16[32,3,192,128]{3,2,1,0:T(8,128)(2,1)}, u32[]{:S(2)}, u32[]{:S(2)}) async-start(bf16[32,3,192,128]{3,2,1,0:T(8,128)(2,1)} %pack_qkg.1), calls=%async_computation | async-start | bytes 9437184 | tf_op jit(solution)/shard_map/all_to_all | solution.py:439
  12.1 0.0 copy-done.3
  12.1 0.1 copy.11
  12.2 0.0 copy-start.2
  12.2 7.2 %pack_v.1 = bf16[32,208,128]{2,1,0:T(8,128)(2,1)} custom-call(s32[1]{0:T(128)} %bitcast.3.parity_ref, bf16[192,4096]{1,0:T(8,128)(2,1)} %v_ref.1, bf16[192,4096]{1,0:T(8,128)(2,1)} %g_ref.3, bf16[192,4096]{1,0:T(8,128)(2,1)} %o_ref.1), custom_call_target="tpu_custom_call" | custom-call | bytes 6291456 | tf_op jit(solution)/shard_map/pack_v/pallas_call | solution.py:120
  19.4 0.0 copy-done.2
  19.4 0.2 convert_reduce_fusion
  19.6 0.1 select_reduce_fusion
  19.7 52.1 %all-to-all-done.x_ref = bf16[32,3,192,128]{3,2,1,0:T(8,128)(2,1)} async-done(((bf16[32,3,192,128]{3,2,1,0:T(8,128)(2,1)}), bf16[32,3,192,128]{3,2,1,0:T(8,128)(2,1)}, u32[]{:S(2)}, u32[]{:S(2)}) %all-to-all-start) | async-done | bytes 4718624 | tf_op jit(solution)/shard_map/all_to_all | solution.py:439
  71.9 4.0 %all-to-all-start.1 = ((bf16[32,208,128]{2,1,0:T(8,128)(2,1)}), bf16[32,208,128]{2,1,0:T(8,128)(2,1)S(1)}, u32[]{:S(2)}, u32[]{:S(2)}) async-start(bf16[32,208,128]{2,1,0:T(8,128)(2,1)} %pack_v.1), calls=%async_computation.1 | async-start | bytes 3407872 | tf_op jit(solution)/shard_map/all_to_all | solution.py:439
  75.9 14.8 %softmax_and_values.1 = (bf16[32,1,192,128]{3,2,1,0:T(8,128)(2,1)}, f32[48,1,128]{2,1,0:T(1,128)S(1)}) custom-call(s32[1,48]{1,0:T(1,128)S(1)} %bitcast.7, s32[48,12]{1,0:T(8,128)S(1)} %bitcast.4, s32[1,48]{1,0:T(1,128)S(1)} %copy-done.2, bf16[32,3,192,128]{3,2,1,0:T(8,128)(2,1)} %all-to-all-done.x_ref), custom_call_target="tpu_custom_call" | custom-call | flops 20000000000 | bytes 6291456 | tf_op jit(solution)/shard_map/softmax_and_values/pallas_call | solution.py:388
  90.6 10.6 %all-to-all-done.1.v_ref = bf16[32,208,128]{2,1,0:T(8,128)(2,1)S(1)} async-done(((bf16[32,208,128]{2,1,0:T(8,128)(2,1)}), bf16[32,208,128]{2,1,0:T(8,128)(2,1)S(1)}, u32[]{:S(2)}, u32[]{:S(2)}) %all-to-all-start.1) | async-done | bytes 1703968 | tf_op jit(solution)/shard_map/all_to_all | solution.py:439
  101.2 4.2 %all-to-all-start.3 = ((bf16[32,1,192,128]{3,2,1,0:T(8,128)(2,1)}), bf16[32,1,192,128]{3,2,1,0:T(8,128)(2,1)S(1)}, u32[]{:S(2)}, u32[]{:S(2)}) async-start(bf16[32,1,192,128]{3,2,1,0:T(8,128)(2,1)} %get-tuple-element.10), calls=%async_computation.3 | async-start | bytes 3145728 | tf_op jit(solution)/shard_map/all_to_all | solution.py:439
  105.4 16.9 %scores_and_gradients.1 = bf16[32,2,192,128]{3,2,1,0:T(8,128)(2,1)} custom-call(s32[1,48]{1,0:T(1,128)S(1)} %bitcast.8, s32[48,12]{1,0:T(8,128)S(1)} %bitcast.5, s32[1,48]{1,0:T(1,128)S(1)} %copy-done.2, bf16[32,3,192,128]{3,2,1,0:T(8,128)(2,1)} %all-to-all-done.x_ref, bf16[32,208,128]{2,1,0:T(8,128)(2,1)S(1)} %all-to-all-done.1.v_ref, ...), custom_call_target="tpu_custom_call" | custom-call | flops 20000000000 | bytes 9437184 | tf_op jit(solution)/shard_map/scores_and_gradients/pallas_call | solution.py:414
  122.3 6.8 %all-to-all-done.3.x_ref = bf16[32,1,192,128]{3,2,1,0:T(8,128)(2,1)S(1)} async-done(((bf16[32,1,192,128]{3,2,1,0:T(8,128)(2,1)}), bf16[32,1,192,128]{3,2,1,0:T(8,128)(2,1)S(1)}, u32[]{:S(2)}, u32[]{:S(2)}) %all-to-all-start.3) | async-done | bytes 1572896 | tf_op jit(solution)/shard_map/all_to_all | solution.py:439
  129.2 0.0 copy-start
  129.2 1.1 copy-done
  130.3 4.6 %all-to-all-start.2 = ((bf16[32,2,192,128]{3,2,1,0:T(8,128)(2,1)}), bf16[32,2,192,128]{3,2,1,0:T(8,128)(2,1)S(1)}, u32[]{:S(2)}, u32[]{:S(2)}) async-start(bf16[32,2,192,128]{3,2,1,0:T(8,128)(2,1)} %scores_and_gradients.1), calls=%async_computation.2 | async-start | bytes 6291456 | tf_op jit(solution)/shard_map/all_to_all | solution.py:439
  134.9 0.0 copy-start.1
  135.0 1.4 copy-done.1
  136.4 2.1 %unpack.3 = bf16[192,4096]{1,0:T(8,128)(2,1)} custom-call(bf16[32,1,192,128]{3,2,1,0:T(8,128)(2,1)S(1)} %copy-done.1), custom_call_target="tpu_custom_call" | custom-call | bytes 3145728 | tf_op jit(solution)/shard_map/unpack/pallas_call | solution.py:158
  138.4 38.3 %all-to-all-done.2.x_ref = bf16[32,2,192,128]{3,2,1,0:T(8,128)(2,1)S(1)} async-done(((bf16[32,2,192,128]{3,2,1,0:T(8,128)(2,1)}), bf16[32,2,192,128]{3,2,1,0:T(8,128)(2,1)S(1)}, u32[]{:S(2)}, u32[]{:S(2)}) %all-to-all-start.2) | async-done | bytes 3145760 | tf_op jit(solution)/shard_map/all_to_all | solution.py:439
  176.7 2.1 %unpack.2 = (bf16[192,4096]{1,0:T(8,128)(2,1)}, bf16[192,4096]{1,0:T(8,128)(2,1)}) custom-call(bf16[32,2,192,128]{3,2,1,0:T(8,128)(2,1)S(1)} %all-to-all-done.2.x_ref), custom_call_target="tpu_custom_call" | custom-call | bytes 6291456 | tf_op jit(solution)/shard_map/unpack/pallas_call | solution.py:158
Async XLA Ops:
  4.6 7.6 %copy-start.3 = (s32[1,48,12]{1,0,2:T(1,128)S(1)}, s32[1,48,12]{1,0,2:T(1,128)}, u32[]{:S(2)}) copy-start(s32[1,48,12]{1,0,2:T(1,128)} %param.12) | copy-start | bytes 6916
  4.6 67.3 %all-to-all-start = ((bf16[32,3,192,128]{3,2,1,0:T(8,128)(2,1)}), bf16[32,3,192,128]{3,2,1,0:T(8,128)(2,1)}, u32[]{:S(2)}, u32[]{:S(2)}) async-start(bf16[32,3,192,128]{3,2,1,0:T(8,128)(2,1)} %pack_qkg.1), calls=%async_computation | async-start | bytes 9437184 | tf_op jit(solution)/shard_map/all_to_all | solution.py:439
  12.2 7.2 %copy-start.2 = (s32[1,48]{1,0:T(1,128)S(1)}, s32[1,48]{1,0:T(1,128)}, u32[]{:S(2)}) copy-start(s32[1,48]{1,0:T(1,128)} %counts.3) | copy-start | bytes 580
  71.9 29.4 %all-to-all-start.1 = ((bf16[32,208,128]{2,1,0:T(8,128)(2,1)}), bf16[32,208,128]{2,1,0:T(8,128)(2,1)S(1)}, u32[]{:S(2)}, u32[]{:S(2)}) async-start(bf16[32,208,128]{2,1,0:T(8,128)(2,1)} %pack_v.1), calls=%async_computation.1 | async-start | bytes 3407872 | tf_op jit(solution)/shard_map/all_to_all | solution.py:439
  101.2 27.9 %all-to-all-start.3 = ((bf16[32,1,192,128]{3,2,1,0:T(8,128)(2,1)}), bf16[32,1,192,128]{3,2,1,0:T(8,128)(2,1)S(1)}, u32[]{:S(2)}, u32[]{:S(2)}) async-start(bf16[32,1,192,128]{3,2,1,0:T(8,128)(2,1)} %get-tuple-element.10), calls=%async_computation.3 | async-start | bytes 3145728 | tf_op jit(solution)/shard_map/all_to_all | solution.py:439
  129.2 1.1 copy-start
  130.3 46.4 %all-to-all-start.2 = ((bf16[32,2,192,128]{3,2,1,0:T(8,128)(2,1)}), bf16[32,2,192,128]{3,2,1,0:T(8,128)(2,1)S(1)}, u32[]{:S(2)}, u32[]{:S(2)}) async-start(bf16[32,2,192,128]{3,2,1,0:T(8,128)(2,1)} %scores_and_gradients.1), calls=%async_computation.2 | async-start | bytes 6291456 | tf_op jit(solution)/shard_map/all_to_all | solution.py:439
  134.9 1.4 copy-start.1

commit v5 on v4

--- a/solution.py
+++ b/solution.py
@@ -11,7 +11,7 @@
 BLK = 128
 SHARDS = 32
 ROWS = 192
-TERMS = 16
+TERMS = 8
 TOKENS = SHARDS * ROWS
 NB = TOKENS // BLK
 KMAX = 12
@@ -112,7 +112,7 @@
             rest = rest - piece
             out = jnp.where(sub == 2 * part, piece[:, :HD], out)
             out = jnp.where(sub == 2 * part + 1, piece[:, HD:], out)
-        x_ref[c, ROWS : ROWS + TERMS] = jnp.concatenate([out, jnp.zeros_like(out)], axis=0).astype(bf16)
+        x_ref[c, ROWS : ROWS + TERMS] = out.astype(bf16)
 
 
 def pack_values(parity, v, g, o):
@@ -182,6 +182,18 @@
         ref[shard, part, pl.ds(start, 64), :] = value[64 * half : 64 * half + 64]
 
 
+def half_rows(ref, piece):
+    shard = (piece * 43) >> 7
+    start = pl.multiple_of((piece - 3 * shard) * 64, 64)
+    return ref[shard, pl.ds(start, 64), :]
+
+
+def gather_shards(ref, blocks, a, slots):
+    return jnp.concatenate(
+        [half_rows(ref, 2 * blocks[a, s] + h) for s in range(slots) for h in range(2)], axis=0
+    )
+
+
 def targets(blocks, a, n, slots):
     return [jnp.where(s < n, blocks[a, s], NB) for s in range(slots)]
 
@@ -313,26 +325,25 @@
 
 def second_kernel(
     order, blocks, counts, x_ref, v_ref, lse_ref, out_ref,
-    q_buf, k_buf, g_buf, v_buf, t_ref, out, acc, kt, terms, ds_ref, wq, wg, wn, in_sem, out_sem,
+    q_buf, k_buf, g_buf, v_buf, out, acc, kt, terms, ds_ref, wq, wg, wn, in_sem, out_sem,
 ):
     k_copy = load(x_ref, 1, k_buf, in_sem.at[0])
-    t_copy = load(v_ref, pl.ds(ROWS, TERMS), t_ref, in_sem.at[1])
+    v_copy = pltpu.make_async_copy(v_ref, v_buf, in_sem.at[1])
+    v_copy.start()
     copies = [
         load(x_ref, 0, q_buf, in_sem.at[2]),
         load(x_ref, 2, g_buf, in_sem.at[3]),
-        load(v_ref, pl.ds(0, ROWS), v_buf, in_sem.at[4]),
     ]
     q = q_buf.reshape(TOKENS, HD)
     k = k_buf.reshape(TOKENS, HD)
     g = g_buf.reshape(TOKENS, HD)
-    v = v_buf.reshape(TOKENS, HD)
     acc[...] = jnp.zeros_like(acc)
     k_copy.wait()
-    t_copy.wait()
+    v_copy.wait()
 
     def row_terms(t, carry):
-        a = t_ref[2 * t].astype(f32)
-        b = t_ref[2 * t + 1].astype(f32)
+        a = v_buf[2 * t, ROWS : ROWS + TERMS].astype(f32)
+        b = v_buf[2 * t + 1, ROWS : ROWS + TERMS].astype(f32)
         a0 = a[0:1] + a[2:3] + a[4:5]
         a1 = a[1:2] + a[3:4] + a[5:6]
         b0 = b[0:1] + b[2:3] + b[4:5]
@@ -358,7 +369,7 @@
         for j in range(GROUP):
             a = ids[j]
             scores = dot(gather(k, blocks, a, slots), wq[slot, j])
-            dp = dot(gather(v, blocks, a, slots), wg[slot, j])
+            dp = dot(gather_shards(v_buf, blocks, a, slots), wg[slot, j])
             lse = lse_ref[a]
             term = terms[a]
             for s in range(slots):
@@ -416,9 +427,9 @@
         in_specs=[SMEM_SPEC] * 3 + [ANY_SPEC] * 2 + [VMEM_SPEC],
         out_specs=HBM_SPEC,
         out_shape=pltpu.HBM((SHARDS, 2, ROWS, HD), bf16),
-        scratch_shapes=[pltpu.VMEM((SHARDS, ROWS, HD), bf16)] * 4
+        scratch_shapes=[pltpu.VMEM((SHARDS, ROWS, HD), bf16)] * 3
         + [
-            pltpu.VMEM((SHARDS, TERMS, HD), bf16),
+            pltpu.VMEM((SHARDS, ROWS + TERMS, HD), bf16),
             pltpu.VMEM((SHARDS, 2, ROWS, HD), bf16),
             pltpu.VMEM((NB + 1, BLK, HD), f32),
             pltpu.VMEM((NB, HD, BLK), bf16),
@@ -426,7 +437,7 @@
             pltpu.VMEM((GROUP, KMAX, BLK, BLK), bf16),
         ]
         + [pltpu.VMEM((2, GROUP, BLK, BLK), bf16)] * 3
-        + [pltpu.SemaphoreType.DMA((5,)), pltpu.SemaphoreType.DMA((OUT_STEPS + 1,))],
+        + [pltpu.SemaphoreType.DMA((4,)), pltpu.SemaphoreType.DMA((OUT_STEPS + 1,))],
         compiler_params=pltpu.CompilerParams(vmem_limit_bytes=40 << 20),
         cost_estimate=pl.CostEstimate(
             flops=20_000_000_000, bytes_accessed=9437184, transcendentals=5_000_000

time: 181 us -> 180 us (level)
  Pallas kernels: 47 us -> 44.7 us
  transfers between devices with their start and end apart: 4 -> 4, of which waited for: 4 -> 4; matrix products, arithmetic and copies ran while one was open for 0% -> 0% of each run, Pallas kernels for 23% -> 22%
where the time goes in v5:
time: 180 us; the launch traced here: 179 us
  waiting for transfers between devices  109 us (61%)
  Pallas kernels  44.7 us (25%)
  starting transfers between devices  21.4 us (12%)
  local copies, waits for them, and re-layouts  2.65 us (1%)
    all_to_all x4, waiting for transfers between devices, exchange(): return lax.all_to_all(x, 'head', split_axis=0, concat_axis=0, tiled=True)  109 us
    all_to_all x4, starting transfers between devices, exchange(): return lax.all_to_all(x, 'head', split_axis=0, concat_axis=0, tiled=True)  21.4 us
    pallas_call x1, Pallas kernels, second_phase(): pl.pallas_call(second_kernel, in_specs=[SMEM_SPEC] * 3 + [ANY_SPEC] * 2 +...  15.8 us
    pallas_call x1, Pallas kernels, first_phase(): pl.pallas_call(first_kernel, in_specs=[SMEM_SPEC] * 3 + [ANY_SPEC], out_s...  13.7 us
    pallas_call x1, Pallas kernels, pack_values(): pl.pallas_call(pack_values_kernel, grid=(SHARDS // COLS,), in_specs=[SMEM...  7.2 us
    pallas_call x2, Pallas kernels, unpack(): pl.pallas_call(functools.partial(unpack_kernel, count), in_specs=[ANY_SPE...  4.13 us
    pallas_call x1, Pallas kernels, pack(): pl.pallas_call(pack_kernel, in_specs=[ANY_SPEC] * 3, out_specs=HBM_SPEC,...  3.93 us
  transfers between devices with their start and end apart: 4, of which 4 were waited for; matrix products, arithmetic and copies ran while one was open for 0% of the time, Pallas kernels for 22%

profile of v5, /device:TPU:0, one launch (start us, length us, event | category | flops | bytes accessed | tf_op | source)
XLA Modules:
  0.0 179.3 jit_solution(14801941758681148026)
XLA Ops:
  0.6 3.9 %pack_qkg.1 = bf16[32,3,192,128]{3,2,1,0:T(8,128)(2,1)} custom-call(bf16[192,4096]{1,0:T(8,128)(2,1)} %q_ref.1, bf16[192,4096]{1,0:T(8,128)(2,1)} %k_ref.1, bf16[192,4096]{1,0:T(8,128)(2,1)} %g_ref.3), custom_call_target="tpu_custom_call" | custom-call | bytes 9437184 | tf_op jit(solution)/shard_map/pack_qkg/pallas_call | solution.py:74
  4.6 0.0 copy-start.3
  4.6 7.5 %all-to-all-start = ((bf16[32,3,192,128]{3,2,1,0:T(8,128)(2,1)}), bf16[32,3,192,128]{3,2,1,0:T(8,128)(2,1)}, u32[]{:S(2)}, u32[]{:S(2)}) async-start(bf16[32,3,192,128]{3,2,1,0:T(8,128)(2,1)} %pack_qkg.1), calls=%async_computation | async-start | bytes 9437184 | tf_op jit(solution)/shard_map/all_to_all | solution.py:450
  12.1 0.0 copy-done.3
  12.1 0.1 copy.11
  12.2 0.0 copy-start.2
  12.2 7.2 %pack_v.1 = bf16[32,200,128]{2,1,0:T(8,128)(2,1)} custom-call(s32[1]{0:T(128)} %bitcast.3.parity_ref, bf16[192,4096]{1,0:T(8,128)(2,1)} %v_ref.1, bf16[192,4096]{1,0:T(8,128)(2,1)} %g_ref.3, bf16[192,4096]{1,0:T(8,128)(2,1)} %o_ref.1), custom_call_target="tpu_custom_call" | custom-call | bytes 6291456 | tf_op jit(solution)/shard_map/pack_v/pallas_call | solution.py:120
  19.4 0.0 copy-done.2
  19.4 0.2 convert_reduce_fusion
  19.6 0.1 select_reduce_fusion
  19.7 52.1 %all-to-all-done.x_ref = bf16[32,3,192,128]{3,2,1,0:T(8,128)(2,1)} async-done(((bf16[32,3,192,128]{3,2,1,0:T(8,128)(2,1)}), bf16[32,3,192,128]{3,2,1,0:T(8,128)(2,1)}, u32[]{:S(2)}, u32[]{:S(2)}) %all-to-all-start) | async-done | bytes 4718624 | tf_op jit(solution)/shard_map/all_to_all | solution.py:450
  71.9 4.0 %all-to-all-start.1 = ((bf16[32,200,128]{2,1,0:T(8,128)(2,1)}), bf16[32,200,128]{2,1,0:T(8,128)(2,1)S(1)}, u32[]{:S(2)}, u32[]{:S(2)}) async-start(bf16[32,200,128]{2,1,0:T(8,128)(2,1)} %pack_v.1), calls=%async_computation.1 | async-start | bytes 3276800 | tf_op jit(solution)/shard_map/all_to_all | solution.py:450
  75.8 13.7 %softmax_and_values.1 = (bf16[32,1,192,128]{3,2,1,0:T(8,128)(2,1)}, f32[48,1,128]{2,1,0:T(1,128)S(1)}) custom-call(s32[1,48]{1,0:T(1,128)S(1)} %bitcast.7, s32[48,12]{1,0:T(8,128)S(1)} %bitcast.4, s32[1,48]{1,0:T(1,128)S(1)} %copy-done.2, bf16[32,3,192,128]{3,2,1,0:T(8,128)(2,1)} %all-to-all-done.x_ref), custom_call_target="tpu_custom_call" | custom-call | flops 20000000000 | bytes 6291456 | tf_op jit(solution)/shard_map/softmax_and_values/pallas_call | solution.py:399
  89.6 10.9 %all-to-all-done.1.v_ref = bf16[32,200,128]{2,1,0:T(8,128)(2,1)S(1)} async-done(((bf16[32,200,128]{2,1,0:T(8,128)(2,1)}), bf16[32,200,128]{2,1,0:T(8,128)(2,1)S(1)}, u32[]{:S(2)}, u32[]{:S(2)}) %all-to-all-start.1) | async-done | bytes 1638432 | tf_op jit(solution)/shard_map/all_to_all | solution.py:450
  100.5 4.2 %all-to-all-start.3 = ((bf16[32,1,192,128]{3,2,1,0:T(8,128)(2,1)}), bf16[32,1,192,128]{3,2,1,0:T(8,128)(2,1)S(1)}, u32[]{:S(2)}, u32[]{:S(2)}) async-start(bf16[32,1,192,128]{3,2,1,0:T(8,128)(2,1)} %get-tuple-element.10), calls=%async_computation.3 | async-start | bytes 3145728 | tf_op jit(solution)/shard_map/all_to_all | solution.py:450
  104.7 15.8 %scores_and_gradients.1 = bf16[32,2,192,128]{3,2,1,0:T(8,128)(2,1)} custom-call(s32[1,48]{1,0:T(1,128)S(1)} %bitcast.8, s32[48,12]{1,0:T(8,128)S(1)} %bitcast.5, s32[1,48]{1,0:T(1,128)S(1)} %copy-done.2, bf16[32,3,192,128]{3,2,1,0:T(8,128)(2,1)} %all-to-all-done.x_ref, bf16[32,200,128]{2,1,0:T(8,128)(2,1)S(1)} %all-to-all-done.1.v_ref, ...), custom_call_target="tpu_custom_call" | custom-call | flops 20000000000 | bytes 9437184 | tf_op jit(solution)/shard_map/scores_and_gradients/pallas_call | solution.py:425
  120.4 8.0 %all-to-all-done.3.x_ref = bf16[32,1,192,128]{3,2,1,0:T(8,128)(2,1)S(1)} async-done(((bf16[32,1,192,128]{3,2,1,0:T(8,128)(2,1)}), bf16[32,1,192,128]{3,2,1,0:T(8,128)(2,1)S(1)}, u32[]{:S(2)}, u32[]{:S(2)}) %all-to-all-start.3) | async-done | bytes 1572896 | tf_op jit(solution)/shard_map/all_to_all | solution.py:450
  128.4 0.0 copy-start
  128.4 1.1 copy-done
  129.6 5.8 %all-to-all-start.2 = ((bf16[32,2,192,128]{3,2,1,0:T(8,128)(2,1)}), bf16[32,2,192,128]{3,2,1,0:T(8,128)(2,1)S(1)}, u32[]{:S(2)}, u32[]{:S(2)}) async-start(bf16[32,2,192,128]{3,2,1,0:T(8,128)(2,1)} %scores_and_gradients.1), calls=%async_computation.2 | async-start | bytes 6291456 | tf_op jit(solution)/shard_map/all_to_all | solution.py:450
  135.3 0.0 copy-start.1
  135.3 1.4 copy-done.1
  136.7 2.1 %unpack.3 = bf16[192,4096]{1,0:T(8,128)(2,1)} custom-call(bf16[32,1,192,128]{3,2,1,0:T(8,128)(2,1)S(1)} %copy-done.1), custom_call_target="tpu_custom_call" | custom-call | bytes 3145728 | tf_op jit(solution)/shard_map/unpack/pallas_call | solution.py:158
  138.8 38.3 %all-to-all-done.2.x_ref = bf16[32,2,192,128]{3,2,1,0:T(8,128)(2,1)S(1)} async-done(((bf16[32,2,192,128]{3,2,1,0:T(8,128)(2,1)}), bf16[32,2,192,128]{3,2,1,0:T(8,128)(2,1)S(1)}, u32[]{:S(2)}, u32[]{:S(2)}) %all-to-all-start.2) | async-done | bytes 3145760 | tf_op jit(solution)/shard_map/all_to_all | solution.py:450
  177.1 2.1 %unpack.2 = (bf16[192,4096]{1,0:T(8,128)(2,1)}, bf16[192,4096]{1,0:T(8,128)(2,1)}) custom-call(bf16[32,2,192,128]{3,2,1,0:T(8,128)(2,1)S(1)} %all-to-all-done.2.x_ref), custom_call_target="tpu_custom_call" | custom-call | bytes 6291456 | tf_op jit(solution)/shard_map/unpack/pallas_call | solution.py:158
Async XLA Ops:
  4.6 7.6 %copy-start.3 = (s32[1,48,12]{1,0,2:T(1,128)S(1)}, s32[1,48,12]{1,0,2:T(1,128)}, u32[]{:S(2)}) copy-start(s32[1,48,12]{1,0,2:T(1,128)} %param.12) | copy-start | bytes 6916
  4.6 67.3 %all-to-all-start = ((bf16[32,3,192,128]{3,2,1,0:T(8,128)(2,1)}), bf16[32,3,192,128]{3,2,1,0:T(8,128)(2,1)}, u32[]{:S(2)}, u32[]{:S(2)}) async-start(bf16[32,3,192,128]{3,2,1,0:T(8,128)(2,1)} %pack_qkg.1), calls=%async_computation | async-start | bytes 9437184 | tf_op jit(solution)/shard_map/all_to_all | solution.py:450
  12.2 7.2 %copy-start.2 = (s32[1,48]{1,0:T(1,128)S(1)}, s32[1,48]{1,0:T(1,128)}, u32[]{:S(2)}) copy-start(s32[1,48]{1,0:T(1,128)} %counts.3) | copy-start | bytes 580
  71.9 28.6 %all-to-all-start.1 = ((bf16[32,200,128]{2,1,0:T(8,128)(2,1)}), bf16[32,200,128]{2,1,0:T(8,128)(2,1)S(1)}, u32[]{:S(2)}, u32[]{:S(2)}) async-start(bf16[32,200,128]{2,1,0:T(8,128)(2,1)} %pack_v.1), calls=%async_computation.1 | async-start | bytes 3276800 | tf_op jit(solution)/shard_map/all_to_all | solution.py:450
  100.5 27.9 %all-to-all-start.3 = ((bf16[32,1,192,128]{3,2,1,0:T(8,128)(2,1)}), bf16[32,1,192,128]{3,2,1,0:T(8,128)(2,1)S(1)}, u32[]{:S(2)}, u32[]{:S(2)}) async-start(bf16[32,1,192,128]{3,2,1,0:T(8,128)(2,1)} %get-tuple-element.10), calls=%async_computation.3 | async-start | bytes 3145728 | tf_op jit(solution)/shard_map/all_to_all | solution.py:450
  128.4 1.1 copy-start
  129.6 47.5 %all-to-all-start.2 = ((bf16[32,2,192,128]{3,2,1,0:T(8,128)(2,1)}), bf16[32,2,192,128]{3,2,1,0:T(8,128)(2,1)S(1)}, u32[]{:S(2)}, u32[]{:S(2)}) async-start(bf16[32,2,192,128]{3,2,1,0:T(8,128)(2,1)} %scores_and_gradients.1), calls=%async_computation.2 | async-start | bytes 6291456 | tf_op jit(solution)/shard_map/all_to_all | solution.py:450
  135.3 1.4 copy-start.1
